TPU v7x, 512 devices: a whole 4x4x16 slice. The times are simulated.
512 devices in a mesh: dp: 8 (over x, core), expert: 64 (over z, y).
Axes of the slice: x: 4, y: 4, z: 16, core: 2. Of those that a mesh axis runs over, the one named last changes fastest.
Arguments:
- tokens: bfloat16 [65536, 512], P(('dp', 'expert')), may hold values from -6 to 6
- expert_ids: int32 [65536, 8], P(('dp', 'expert')), may hold values from 0 to 63, all different within a row; in each aligned block of 128 rows (0 to 127, 128 to 255, ...) at most 20 rows name the same one
- gate_weights: float32 [65536, 8], P(('dp', 'expert')), may hold values from 0.1 to 1
- cotangent: bfloat16 [65536, 512], P(('dp', 'expert')), may hold values from -6 to 6
- w_gate: bfloat16 [64, 512, 512], P('expert'), may hold values from -0.25 to 0.25
- w_up: bfloat16 [64, 512, 512], P('expert'), may hold values from -0.25 to 0.25
- w_down: bfloat16 [64, 512, 512], P('expert'), may hold values from -0.25 to 0.25
Outputs:
- layer_out: bfloat16 [65536, 512], P(('dp', 'expert'))
- grad_tokens: bfloat16 [65536, 512], P(('dp', 'expert'))
- grad_gates: float32 [65536, 8], P(('dp', 'expert'))
- grad_w_gate: bfloat16 [64, 512, 512], P('expert')
- grad_w_up: bfloat16 [64, 512, 512], P('expert')
- grad_w_down: bfloat16 [64, 512, 512], P('expert')
Inputs may be any that keep to these rules, and one draw needn't show every extreme that they name: `expert_ids`: each row names 8 different experts. Among the 128 rows of one device no expert is named by more than 20 rows, a bound that some block reaches.
All inputs are finite; a program needn't handle non-finite values.
Results may differ from a plain program's by a relative error of at most 0.0064.
Values may be sent and summed in bfloat16 or wider, within the bound.
No kernel may reach another device: no remote copies, remote signals or barrier semaphores. Data moves between devices by JAX's collectives and lax.ppermute only.
A program may use at most 64 MiB of HBM per device.

v0:
```python
import jax
import jax.numpy as jnp
from jax import lax
from jax.sharding import PartitionSpec as P


def silu_parts(pre_act):
    sigmoid_val = jax.nn.sigmoid(pre_act)
    return (pre_act * sigmoid_val, sigmoid_val * (1.0 + pre_act * (1.0 - sigmoid_val)))


def body(tokens, expert_ids, gate_weights, cotangent, w_gate, w_up, w_down):
    tok_rows = tokens.shape[0]
    feature_width = tokens.shape[1]
    top_count = expert_ids.shape[1]
    local_experts = w_gate.shape[0]
    hidden_width = w_gate.shape[2]
    expert_total = local_experts * lax.axis_size("expert")
    slot_count = tok_rows * top_count * 5 // (expert_total * 4)
    flat_ids = expert_ids.reshape(-1)
    onehot = (flat_ids[:, None] == jnp.arange(expert_total, dtype=jnp.int32)[None, :]).astype(
        jnp.int32
    )
    slot_index = jnp.sum((jnp.cumsum(onehot, axis=0) - onehot) * onehot, axis=1)
    target = flat_ids * slot_count + slot_index

    def to_slots(row_values):
        buffer = jnp.zeros((expert_total * slot_count, feature_width), jnp.bfloat16)
        return buffer.at[target].set(row_values).reshape(expert_total, slot_count, feature_width)

    def from_slots(buffer):
        picked = buffer.reshape(-1, feature_width)[target]
        return picked.reshape(tok_rows, top_count, feature_width).astype(jnp.float32)

    def by_expert(values):
        return values.reshape(-1, local_experts, values.shape[1], values.shape[2])

    row_values = jnp.broadcast_to(tokens[:, None, :], (tok_rows, top_count, feature_width)).reshape(
        -1, feature_width
    )
    cot_wide = cotangent.astype(jnp.float32)
    out_grad = (
        (gate_weights[:, :, None] * cot_wide[:, None, :])
        .astype(jnp.bfloat16)
        .reshape(-1, feature_width)
    )
    received = lax.all_to_all(
        to_slots(row_values), "expert", split_axis=0, concat_axis=0, tiled=True
    )
    item_count = received.shape[1]
    grouped = by_expert(received)
    gate_pre = jnp.einsum("secl,elh->sech", grouped, w_gate, preferred_element_type=jnp.float32)
    up_pre = jnp.einsum("secl,elh->sech", grouped, w_up, preferred_element_type=jnp.float32)
    activation, derivative = silu_parts(gate_pre)
    hidden = (activation * up_pre).astype(jnp.bfloat16)
    expert_out = jnp.einsum(
        "sech,ehl->secl", hidden, w_down, preferred_element_type=jnp.float32
    ).astype(jnp.bfloat16)
    expert_out, activation, derivative, up_pre, hidden = (
        expert_out,
        activation,
        derivative,
        up_pre,
        hidden,
    )
    flat_shape = (-1, item_count, hidden_width)
    expert_out, rows_in, activation, derivative, up_pre, hidden = (
        expert_out.reshape(received.shape),
        received,
        activation.reshape(flat_shape),
        derivative.reshape(flat_shape),
        up_pre.reshape(flat_shape),
        hidden.reshape(flat_shape),
    )
    returned = lax.all_to_all(expert_out, "expert", split_axis=0, concat_axis=0, tiled=True)
    grad_in = by_expert(
        lax.all_to_all(to_slots(out_grad), "expert", split_axis=0, concat_axis=0, tiled=True)
    )
    backward_activation = by_expert(activation)
    backward_derivative = by_expert(derivative)
    backward_up_pre = by_expert(up_pre)
    hidden_grad = jnp.einsum("secl,ehl->sech", grad_in, w_down, preferred_element_type=jnp.float32)
    gate_back = (hidden_grad * backward_up_pre * backward_derivative).astype(jnp.bfloat16)
    up_back = (hidden_grad * backward_activation).astype(jnp.bfloat16)
    input_back = jnp.einsum(
        "sech,elh->secl", gate_back, w_gate, preferred_element_type=jnp.float32
    ) + jnp.einsum("sech,elh->secl", up_back, w_up, preferred_element_type=jnp.float32)
    input_back, gate_back, up_back = (input_back.astype(jnp.bfloat16), gate_back, up_back)
    input_back = input_back.reshape(expert_total, slot_count, feature_width)
    returned_grads = lax.all_to_all(input_back, "expert", split_axis=0, concat_axis=0, tiled=True)
    out_rows = from_slots(returned)
    layer_out = jnp.sum(gate_weights[:, :, None] * out_rows, axis=1).astype(jnp.bfloat16)
    grad_gates = jnp.sum(cot_wide[:, None, :] * out_rows, axis=2)
    grad_tokens = jnp.sum(from_slots(returned_grads), axis=1).astype(jnp.bfloat16)
    grouped_in = by_expert(rows_in)
    grad_gate_part = jnp.einsum(
        "secl,sech->elh", grouped_in, gate_back, preferred_element_type=jnp.float32
    )
    grad_up_part = jnp.einsum(
        "secl,sech->elh", grouped_in, up_back, preferred_element_type=jnp.float32
    )
    grad_down_part = jnp.einsum(
        "sech,secl->ehl", by_expert(hidden), grad_in, preferred_element_type=jnp.float32
    )
    grad_scale = float(
        lax.axis_size("dp") * tok_rows * top_count * lax.axis_size("expert") // expert_total
    ) ** (-0.5)
    totals = lax.psum((grad_gate_part, grad_up_part, grad_down_part), "dp")
    grad_w_gate = (totals[0] * grad_scale).astype(jnp.bfloat16)
    grad_w_up = (totals[1] * grad_scale).astype(jnp.bfloat16)
    grad_w_down = (totals[2] * grad_scale).astype(jnp.bfloat16)
    return (layer_out, grad_tokens, grad_gates, grad_w_gate, grad_w_up, grad_w_down)


def solution(mesh):
    placed = (
        P(("dp", "expert"), None),
        P(("dp", "expert"), None),
        P(("dp", "expert"), None),
        P(("dp", "expert"), None),
        P("expert", None, None),
        P("expert", None, None),
        P("expert", None, None),
    )
    return jax.shard_map(
        body,
        mesh=mesh,
        in_specs=placed,
        out_specs=(
            P(("dp", "expert"), None),
            P(("dp", "expert"), None),
            P(("dp", "expert"), None),
            P("expert", None, None),
            P("expert", None, None),
            P("expert", None, None),
        ),
        check_vma=False,
    )
```

profile of v0, /device:TPU:6, one launch (start us, length us, event | category | flops | bytes accessed | tf_op | source)
XLA Modules:
  0.0 431.3 jit_solution(579931842196189963)
XLA Ops:
  9.1 18.0 %reduce-window.6 = s32[64,8,128]{2,1,0:T(8,128)S(1)} reduce-window(s32[64,8,128]{2,1,0:T(8,128)S(1)} %fusion.44, s32[]{:T(128)} %constant.4.clone.1), window={size=1x1x128 pad=0_0x0_0x127_0}, to_apply=%region_0.0 | reduce-window | flops 8323072 | bytes 524292 | tf_op jit(solution)/shard_map/reduce-window
  27.8 5.5 %scatter_custom_fusion = bf16[1280,512]{1,0:T(8,128)(2,1)S(1)} fusion(s32[1024]{0:T(1024)S(1)} %bitcast.135, bf16[]{:T(256)} %constant.7.clone.1, bf16[128,512]{1,0:T(8,128)(2,1)S(1)} %copy-done.13), kind=kCustom, calls=%fused_computation.37 | custom fusion | bytes 1441794 | tf_op jit(solution)/shard_map/scatter | solution.py:29
  34.6 18.9 %all-to-all-start = ((bf16[64,20,512]{2,1,0:T(8,128)(2,1)}), bf16[64,20,512]{2,1,0:T(8,128)(2,1)S(1)}, u32[]{:S(2)}, u32[]{:S(2)}) async-start(bf16[64,20,512]{2,1,0:T(8,128)(2,1)} %reshape.150), calls=%async_computation | async-start | bytes 3145728 | tf_op jit(solution)/shard_map/all_to_all | solution.py:47
  54.4 6.2 %scatter_custom_fusion.1 = bf16[1280,512]{1,0:T(8,128)(2,1)S(1)} fusion(s32[1024]{0:T(1024)S(1)} %bitcast.136, f32[128,512]{1,0:T(8,128)} %convert_element_type.66, f32[1024]{0:T(1024)S(1)} %mul.93, bf16[]{:T(256)} %constant.7.clone.1), kind=kCustom, calls=%fused_computation.35 | custom fusion | flops 1048576 | bytes 1576962 | tf_op jit(solution)/shard_map/scatter | solution.py:29
  61.9 69.3 %all-to-all-done = bf16[64,20,512]{2,1,0:T(8,128)(2,1)S(1)} async-done(((bf16[64,20,512]{2,1,0:T(8,128)(2,1)}), bf16[64,20,512]{2,1,0:T(8,128)(2,1)S(1)}, u32[]{:S(2)}, u32[]{:S(2)}) %all-to-all-start) | async-done | bytes 1310752 | tf_op jit(solution)/shard_map/all_to_all | solution.py:47
  131.2 6.2 %all-to-all-start.2 = ((bf16[64,20,512]{2,1,0:T(8,128)(2,1)}), bf16[64,20,512]{2,1,0:T(8,128)(2,1)}, u32[]{:S(2)}, u32[]{:S(2)}) async-start(bf16[64,20,512]{2,1,0:T(8,128)(2,1)} %reshape.156), calls=%async_computation.2 | async-start | bytes 3145728 | tf_op jit(solution)/shard_map/all_to_all | solution.py:77
  137.5 2.4 fusion.31
  139.9 74.5 %all-to-all-done.2 = bf16[64,20,512]{2,1,0:T(8,128)(2,1)} async-done(((bf16[64,20,512]{2,1,0:T(8,128)(2,1)}), bf16[64,20,512]{2,1,0:T(8,128)(2,1)}, u32[]{:S(2)}, u32[]{:S(2)}) %all-to-all-start.2) | async-done | bytes 1310752 | tf_op jit(solution)/shard_map/all_to_all | solution.py:77
  214.4 2.4 fusion.24
  216.9 3.3 fusion.13
  222.6 1.9 copy.36
  224.5 5.8 %all-to-all-start.3 = ((bf16[64,20,512]{2,1,0:T(8,128)(2,1)}), bf16[64,20,512]{2,1,0:T(8,128)(2,1)S(1)}, u32[]{:S(2)}, u32[]{:S(2)}) async-start(bf16[64,20,512]{2,1,0:T(8,128)(2,1)} %copy.36), calls=%async_computation.3 | async-start | bytes 3145728 | tf_op jit(solution)/shard_map/all_to_all | solution.py:90
  230.4 2.2 convolution_convert_fusion
  234.4 72.9 %all-to-all-done.3 = bf16[64,20,512]{2,1,0:T(8,128)(2,1)S(1)} async-done(((bf16[64,20,512]{2,1,0:T(8,128)(2,1)}), bf16[64,20,512]{2,1,0:T(8,128)(2,1)S(1)}, u32[]{:S(2)}, u32[]{:S(2)}) %all-to-all-start.3) | async-done | bytes 1310752 | tf_op jit(solution)/shard_map/all_to_all | solution.py:90
  307.3 6.1 %all-to-all-start.1 = ((bf16[64,20,512]{2,1,0:T(8,128)(2,1)}), bf16[64,20,512]{2,1,0:T(8,128)(2,1)}, u32[]{:S(2)}, u32[]{:S(2)}) async-start(bf16[64,20,512]{2,1,0:T(8,128)(2,1)} %copy.33), calls=%async_computation.1 | async-start | bytes 3145728 | tf_op jit(solution)/shard_map/all_to_all | solution.py:75
  313.6 3.8 convolution_bitcast_fusion
  317.5 1.9 convolution_bitcast_fusion.1
  319.4 1.9 convolution_bitcast_fusion.2
  321.3 84.3 %all-reduce.3.cloned.1.call-done = (f32[1,512,512]{2,1,0:T(8,128)}, f32[1,512,512]{2,1,0:T(8,128)}, f32[1,512,512]{2,1,0:T(8,128)}) async-done(((f32[1,512,512]{2,1,0:T(8,128)}, f32[1,512,512]{2,1,0:T(8,128)}, f32[1,512,512]{2,1,0:T(8,128)}), (f32[1,512,512]{2,1,0:T(8,128)}, f32[1,512,512]{2,1,0:T(8,128)}, f32[1,512,512]{2,1,0:T(8,128)})) %all-reduce.3.cloned.1.call-update) | async-done | bytes 3145744 | tf_op jit(solution)/shard_map/psum | solution.py:108
  405.6 2.2 multiply_convert_fusion.2
  407.8 2.5 multiply_convert_fusion
  410.6 4.0 gather_fusion.1
  415.9 2.3 reshape.155
  418.2 4.0 gather_fusion
  (61 shorter events, 14.6 us)
Async XLA Ops:
  7.2 209.7 %copy-start = (bf16[1,512,512]{2,1,0:T(8,128)(2,1)S(1)}, bf16[1,512,512]{2,1,0:T(8,128)(2,1)}, u32[]{:S(2)}) copy-start(bf16[1,512,512]{2,1,0:T(8,128)(2,1)} %param.11) | copy-start | bytes 1572868
  8.9 18.9 %copy-start.13 = (bf16[128,512]{1,0:T(8,128)(2,1)S(1)}, bf16[128,512]{1,0:T(8,128)(2,1)}, u32[]{:S(2)}) copy-start(bf16[128,512]{1,0:T(8,128)(2,1)} %param.7) | copy-start | bytes 393220
  34.6 18.9 %copy-start.14 = (f32[128,8]{0,1:T(8,128)S(1)}, f32[128,8]{0,1:T(8,128)}, u32[]{:S(2)}) copy-start(f32[128,8]{0,1:T(8,128)} %param.9) | copy-start | bytes 12292
  34.6 19.1 %copy-start.12 = (bf16[128,512]{1,0:T(8,128)(2,1)S(1)}, bf16[128,512]{1,0:T(8,128)(2,1)}, u32[]{:S(2)}) copy-start(bf16[128,512]{1,0:T(8,128)(2,1)} %param.10) | copy-start | bytes 393220
  34.6 96.6 %all-to-all-start = ((bf16[64,20,512]{2,1,0:T(8,128)(2,1)}), bf16[64,20,512]{2,1,0:T(8,128)(2,1)S(1)}, u32[]{:S(2)}, u32[]{:S(2)}) async-start(bf16[64,20,512]{2,1,0:T(8,128)(2,1)} %reshape.150), calls=%async_computation | async-start | bytes 3145728 | tf_op jit(solution)/shard_map/all_to_all | solution.py:47
  61.9 75.6 %copy-start.5 = (bf16[1,512,512]{2,1,0:T(8,128)(2,1)S(1)}, bf16[1,512,512]{2,1,0:T(8,128)(2,1)}, u32[]{:S(2)}) copy-start(bf16[1,512,512]{2,1,0:T(8,128)(2,1)} %param.12) | copy-start | bytes 1572868
  131.2 85.6 %copy-start.1 = (bf16[64,20,512]{2,1,0:T(8,128)(2,1)}, bf16[64,20,512]{2,1,0:T(8,128)(2,1)S(1)}, u32[]{:S(2)}) copy-start(bf16[64,20,512]{2,1,0:T(8,128)(2,1)S(1)} %all-to-all-done) | copy-start | bytes 3932164
  131.2 83.2 %all-to-all-start.2 = ((bf16[64,20,512]{2,1,0:T(8,128)(2,1)}), bf16[64,20,512]{2,1,0:T(8,128)(2,1)}, u32[]{:S(2)}, u32[]{:S(2)}) async-start(bf16[64,20,512]{2,1,0:T(8,128)(2,1)} %reshape.156), calls=%async_computation.2 | async-start | bytes 3145728 | tf_op jit(solution)/shard_map/all_to_all | solution.py:77
  137.5 76.9 %copy-start.11 = (bf16[1,512,512]{2,1,0:T(8,128)(2,1)S(1)}, bf16[1,512,512]{2,1,0:T(8,128)(2,1)}, u32[]{:S(2)}) copy-start(bf16[1,512,512]{2,1,0:T(8,128)(2,1)} %param.13) | copy-start | bytes 1572868
  214.4 2.5 copy-start.3
  220.2 1.1 copy-start.6
  220.2 1.5 copy-start.8
  224.5 82.8 %all-to-all-start.3 = ((bf16[64,20,512]{2,1,0:T(8,128)(2,1)}), bf16[64,20,512]{2,1,0:T(8,128)(2,1)S(1)}, u32[]{:S(2)}, u32[]{:S(2)}) async-start(bf16[64,20,512]{2,1,0:T(8,128)(2,1)} %copy.36), calls=%async_computation.3 | async-start | bytes 3145728 | tf_op jit(solution)/shard_map/all_to_all | solution.py:90
  307.3 108.7 %all-to-all-start.1 = ((bf16[64,20,512]{2,1,0:T(8,128)(2,1)}), bf16[64,20,512]{2,1,0:T(8,128)(2,1)}, u32[]{:S(2)}, u32[]{:S(2)}) async-start(bf16[64,20,512]{2,1,0:T(8,128)(2,1)} %copy.33), calls=%async_computation.1 | async-start | bytes 3145728 | tf_op jit(solution)/shard_map/all_to_all | solution.py:75
  313.4 4.1 copy-start.9
  313.4 92.2 %all-reduce.3.cloned.1.call-start = ((), (), s32[]{:S(2)}) async-start(), calls=%async_computation.4 | async-start | bytes 6291456 | tf_op jit(solution)/shard_map/psum | solution.py:108
  313.6 3.8 copy-start.2
  317.5 1.9 copy-start.7
  405.6 2.2 copy-start.10
  418.2 4.0 copy-start.4
Sparse Core Ops, SparseCore 0:
  321.5 84.0 all-reduce.2
where the time goes:
time: 434 us; the launch traced here: 431 us
  waiting for transfers between devices  301 us (69%)
  starting transfers between devices  37.3 us (9%)
  other arithmetic  33.6 us (8%)
  local copies, waits for them, and re-layouts  25.4 us (6%)
  matrix products  19.7 us (5%)
  between operations  14.3 us (3%)
    psum x1, waiting for transfers between devices, body(): totals = lax.psum((grad_gate_part, grad_up_part, grad_down_part), 'dp')  84.3 us
    all_to_all x1, waiting for transfers between devices, body(): lax.all_to_all(to_slots(out_grad), 'expert', split_axis=0, concat_axis=0,...  74.5 us
    all_to_all x1, waiting for transfers between devices, body(): lax.all_to_all(input_back, 'expert', split_axis=0, concat_axis=0, tiled=T...  72.9 us
    all_to_all x1, waiting for transfers between devices, body(): lax.all_to_all(to_slots(row_values), 'expert', split_axis=0, concat_axis=...  69.3 us
    all_to_all x1, starting transfers between devices, body(): lax.all_to_all(to_slots(row_values), 'expert', split_axis=0, concat_axis=...  18.9 us
    another operation x3, other arithmetic  18.2 us
  transfers between devices with their start and end apart: 5, of which 4 were waited for; matrix products, arithmetic and copies ran while one was open for 8% of the time, Pallas kernels for 0%

commit v1 on v0

v1 whole, which is shorter than its diff:
```python
import functools
import jax
import jax.numpy as jnp
from jax import lax
from jax.experimental import pallas as pl
from jax.experimental.pallas import tpu as pltpu
from jax.sharding import Mesh, PartitionSpec as P

BF = jnp.bfloat16
F32 = jnp.float32
TOK = 128
WIDTH = 512
TOP = 8
CAP = 20
HI = 8
LO = 8
PACK = 4
GROUPS = HI // PACK
SLOTS = PACK * CAP
GTOK = PACK * TOK
LANES = 128
CUTS = WIDTH // LANES
SENT = 2 * WIDTH + 4 * TOP
BACK = 2 * WIDTH + 2 * TOP
ROWS = HI * CAP * LO
PARAMS = pltpu.CompilerParams(vmem_limit_bytes=56 * 1024 * 1024)
VMEM = pl.BlockSpec(memory_space=pltpu.VMEM)
SMEM = pl.BlockSpec(memory_space=pltpu.SMEM)


def nn(a, b):
    return jnp.dot(a, b, preferred_element_type=F32)


def nt(a, b):
    return lax.dot_general(a, b, (((1,), (1,)), ((), ())), preferred_element_type=F32)


def tn(a, b):
    return lax.dot_general(a, b, (((0,), (0,)), ((), ())), preferred_element_type=F32)


def call(kernel, shapes, args, scratch=(), scalars=0, flops=0):
    moved = sum(a.size * a.dtype.itemsize for a in args)
    moved += sum(s.size * s.dtype.itemsize for s in shapes)
    return pl.pallas_call(
        kernel,
        out_shape=shapes,
        in_specs=[SMEM] * scalars + [VMEM] * (len(args) - scalars),
        out_specs=[VMEM] * len(shapes),
        scratch_shapes=list(scratch),
        compiler_params=PARAMS,
        cost_estimate=pl.CostEstimate(flops=flops, bytes_accessed=moved, transcendentals=0),
    )(*args)


def pack_kernel(tok, ids, gates, cot, out):
    for f in range(CUTS):
        cut = slice(f * LANES, (f + 1) * LANES)
        out[f * TOK : (f + 1) * TOK, :] = tok[:, cut]
        out[WIDTH + f * TOK : WIDTH + (f + 1) * TOK, :] = cot[:, cut]
    gate = gates[...]
    high = gate.astype(BF).astype(F32)
    middle = (gate - high).astype(BF).astype(F32)
    low = gate - high - middle
    at = 2 * WIDTH
    out[at : at + 16, :] = jnp.concatenate([ids[...].astype(F32), high], axis=0).astype(BF)
    out[at + 16 : at + 32, :] = jnp.concatenate([middle, low], axis=0).astype(BF)


def group_rows(ref, group, first, count):
    parts = []
    for b in range(PACK):
        at = (group * PACK + b) * SENT + first
        parts.append(ref[at : at + count, :].astype(F32))
    return jnp.concatenate(parts, axis=1)


def dispatch_kernel(first, got, x_out, og_out, rank_out, gate_out, tok_s, cot_s):
    base = (first[0] * LO).astype(F32)
    row = lax.broadcasted_iota(jnp.int32, (GTOK, GTOK), 0)
    col = lax.broadcasted_iota(jnp.int32, (GTOK, GTOK), 1)
    upto = (row <= col).astype(F32).astype(BF)
    place = (lax.broadcasted_iota(jnp.int32, (SLOTS, GTOK), 0) + 1).astype(F32)
    for g in range(GROUPS):
        for b in range(PACK):
            at = (g * PACK + b) * SENT
            for f in range(CUTS):
                cut = slice(f * LANES, (f + 1) * LANES)
                rows = slice(b * TOK, (b + 1) * TOK)
                tok_s[rows, cut] = got[at + f * TOK : at + (f + 1) * TOK, :]
                cot_s[rows, cut] = got[at + WIDTH + f * TOK : at + WIDTH + (f + 1) * TOK, :]
        ids_high = group_rows(got, g, 2 * WIDTH, 16)
        middle_low = group_rows(got, g, 2 * WIDTH + 16, 16)
        ids = ids_high[:TOP]
        gates = (ids_high[TOP:] + middle_low[:TOP]) + middle_low[TOP:]
        named, weight = [], []
        for e in range(LO):
            same = ids == base + e
            named.append(jnp.sum(jnp.where(same, 1.0, 0.0), axis=0, keepdims=True))
            weight.append(jnp.sum(jnp.where(same, gates, 0.0), axis=0, keepdims=True))
        named = jnp.concatenate(named, axis=0)
        rank_out[g * LO : (g + 1) * LO, :] = named * nn(named.astype(BF), upto)
        gate_out[g * LO : (g + 1) * LO, :] = jnp.concatenate(weight, axis=0)

        def one(e, carry):
            picks = rank_out[pl.ds(g * LO + e, 1), :] == place
            picked = jnp.where(picks, 1.0, 0.0).astype(BF)
            to = pl.ds(pl.multiple_of((e * GROUPS + g) * SLOTS, 16), SLOTS)
            x_out[to, :] = nn(picked, tok_s[...]).astype(BF)
            gate = jnp.where(picks, gate_out[pl.ds(g * LO + e, 1), :], 0.0)
            og_out[to, :] = (
                jnp.sum(gate, axis=1, keepdims=True) * nn(picked, cot_s[...])
            ).astype(BF)
            return carry

        lax.fori_loop(0, LO, one, 0)


TILE = 160


def forward_kernel(x, w_gate, w_up, w_down, out, hidden, act, slope):
    def one(i, carry):
        rows = pl.ds(pl.multiple_of(i * TILE, 16), TILE)
        gate_pre = nn(x[rows, :], w_gate[...])
        up_pre = nn(x[rows, :], w_up[...])
        sig = jax.nn.sigmoid(gate_pre)
        activation = gate_pre * sig
        mixed = (activation * up_pre).astype(BF)
        hidden[rows, :] = mixed
        act[rows, :] = activation
        slope[rows, :] = up_pre * (sig * (1.0 + gate_pre * (1.0 - sig)))
        out[rows, :] = nn(mixed, w_down[...]).astype(BF)
        return carry

    lax.fori_loop(0, ROWS // TILE, one, 0)


def backward_kernel(og, act, slope, w_gate, w_up, w_down, out, gate_back, up_back):
    def one(i, carry):
        rows = pl.ds(pl.multiple_of(i * TILE, 16), TILE)
        hidden_grad = nt(og[rows, :], w_down[...])
        gate = (hidden_grad * slope[rows, :]).astype(BF)
        up = (hidden_grad * act[rows, :]).astype(BF)
        gate_back[rows, :] = gate
        up_back[rows, :] = up
        out[rows, :] = (nt(gate, w_gate[...]) + nt(up, w_up[...])).astype(BF)
        return carry

    lax.fori_loop(0, ROWS // TILE, one, 0)


def weight_kernel(x, og, hidden, gate_back, up_back, out):
    out[0:WIDTH, :] = tn(x[...], gate_back[...]).astype(BF)
    out[WIDTH : 2 * WIDTH, :] = tn(x[...], up_back[...]).astype(BF)
    out[2 * WIDTH : 3 * WIDTH, :] = tn(hidden[...], og[...]).astype(BF)


def split(value):
    high = value.astype(BF)
    return high, (value - high.astype(F32)).astype(BF)


def combine_kernel(first, got, rank, gate, eo, ib, out, cot_s, eo_s, ib_s):
    base = (first[0] * LO).astype(F32)
    slots = LO * SLOTS
    expert = lax.broadcasted_iota(jnp.int32, (LO, slots), 0)
    slot = lax.broadcasted_iota(jnp.int32, (LO, slots), 1)
    spread = ((slot >= expert * SLOTS) & (slot < (expert + 1) * SLOTS)).astype(F32).astype(BF)
    lane = lax.broadcasted_iota(jnp.int32, (1, slots), 1)
    place = (lane - SLOTS * lax.div(lane, SLOTS) + 1).astype(F32)
    for g in range(GROUPS):
        for b in range(PACK):
            at = (g * PACK + b) * SENT + WIDTH
            for f in range(CUTS):
                cot_s[b * TOK : (b + 1) * TOK, f * LANES : (f + 1) * LANES] = got[
                    at + f * TOK : at + (f + 1) * TOK, :
                ]
        for e in range(LO):
            at = (e * GROUPS + g) * SLOTS
            eo_s[e * SLOTS : (e + 1) * SLOTS, :] = eo[at : at + SLOTS, :]
            ib_s[e * SLOTS : (e + 1) * SLOTS, :] = ib[at : at + SLOTS, :]
        rows = slice(g * LO, (g + 1) * LO)
        ranks = tn(rank[rows, :].astype(BF), spread)
        picks = ranks == place
        high, low = split(gate[rows, :])
        high = jnp.where(picks, tn(high, spread), 0.0).astype(BF)
        low = jnp.where(picks, tn(low, spread), 0.0).astype(BF)
        layer = nn(high, eo_s[...]) + nn(low, eo_s[...])
        back = nn(jnp.where(picks, 1.0, 0.0).astype(BF), ib_s[...])
        along = jnp.where(picks, nt(cot_s[...], eo_s[...]), 0.0)
        high, low = split(along)
        along = nt(spread, high) + nt(spread, low)
        ids = group_rows(got, g, 2 * WIDTH, 16)[:TOP]
        grad = jnp.zeros((TOP, GTOK), F32)
        for e in range(LO):
            grad += jnp.where(ids == base + e, along[e : e + 1, :], 0.0)
        grad_high = grad.astype(BF).astype(F32)
        grad = jnp.concatenate([grad_high, grad - grad_high], axis=0).astype(BF)
        for b in range(PACK):
            at = (g * PACK + b) * BACK
            for f in range(CUTS):
                here = (slice(b * TOK, (b + 1) * TOK), slice(f * LANES, (f + 1) * LANES))
                out[at + f * TOK : at + (f + 1) * TOK, :] = layer[here].astype(BF)
                out[at + WIDTH + f * TOK : at + WIDTH + (f + 1) * TOK, :] = back[here].astype(BF)
            out[at + 2 * WIDTH : at + BACK, :] = grad[:, b * TOK : (b + 1) * TOK]


def unpack_kernel(got, layer, back, grad):
    for f in range(CUTS):
        cut = slice(f * LANES, (f + 1) * LANES)
        layer[:, cut] = got[f * TOK : (f + 1) * TOK, :]
        back[:, cut] = got[WIDTH + f * TOK : WIDTH + (f + 1) * TOK, :]
    parts = got[2 * WIDTH : BACK, :].astype(F32)
    grad[...] = parts[:TOP] + parts[TOP:]


def body(tokens, expert_ids, gate_weights, cotangent, w_gate, w_up, w_down):
    shape = jax.ShapeDtypeStruct
    first = lax.axis_index("hi").astype(jnp.int32).reshape(1)
    w_gate, w_up, w_down = w_gate[0], w_up[0], w_down[0]
    square = 2 * ROWS * WIDTH * WIDTH
    (packed,) = call(
        pack_kernel,
        [shape((SENT, LANES), BF)],
        [tokens, expert_ids.T, gate_weights.T, cotangent],
    )
    got = lax.all_gather(packed, "hi", axis=0, tiled=True)
    rows_in, out_grad, rank, gate = call(
        dispatch_kernel,
        [
            shape((ROWS, WIDTH), BF),
            shape((ROWS, WIDTH), BF),
            shape((GROUPS * LO, GTOK), F32),
            shape((GROUPS * LO, GTOK), F32),
        ],
        [first, got],
        [pltpu.VMEM((GTOK, WIDTH), BF), pltpu.VMEM((GTOK, WIDTH), BF)],
        scalars=1,
        flops=2 * square,
    )
    exchange = functools.partial(
        lax.all_to_all, axis_name="lo", split_axis=0, concat_axis=0, tiled=True
    )
    x = exchange(rows_in)
    og = exchange(out_grad)
    wide = shape((ROWS, WIDTH), F32)
    narrow = shape((ROWS, WIDTH), BF)
    expert_out, hidden, act, slope = call(
        forward_kernel,
        [narrow, narrow, wide, wide],
        [x, w_gate, w_up, w_down],
        flops=3 * square,
    )
    eo = exchange(expert_out)
    input_back, gate_back, up_back = call(
        backward_kernel,
        [narrow, narrow, narrow],
        [og, act, slope, w_gate, w_up, w_down],
        flops=3 * square,
    )
    ib = exchange(input_back)
    (weight_part,) = call(
        weight_kernel,
        [shape((3 * WIDTH, WIDTH), BF)],
        [x, og, hidden, gate_back, up_back],
        flops=3 * square,
    )
    (partial,) = call(
        combine_kernel,
        [shape((HI * BACK, LANES), BF)],
        [first, got, rank, gate, eo, ib],
        [
            pltpu.VMEM((GTOK, WIDTH), BF),
            pltpu.VMEM((LO * SLOTS, WIDTH), BF),
            pltpu.VMEM((LO * SLOTS, WIDTH), BF),
        ],
        scalars=1,
        flops=4 * square,
    )
    summed = lax.psum_scatter(partial, "hi", scatter_dimension=0, tiled=True)
    over_dp = functools.partial(
        lax.all_to_all, axis_name="dp", split_axis=0, concat_axis=0, tiled=True
    )
    data = lax.axis_size("dp")
    share = over_dp(weight_part).reshape(data, -1, WIDTH).astype(F32)
    grad_scale = float(data * TOK * TOP) ** (-0.5)
    share = (jnp.sum(share, axis=0) * grad_scale).astype(BF)
    weight_grad = over_dp(jnp.tile(share, (data, 1))).reshape(3, 1, WIDTH, WIDTH)
    layer_out, grad_tokens, grad_gates = call(
        unpack_kernel,
        [shape((TOK, WIDTH), BF), shape((TOK, WIDTH), BF), shape((TOP, LANES), F32)],
        [summed],
    )
    return (
        layer_out,
        grad_tokens,
        grad_gates.T,
        weight_grad[0],
        weight_grad[1],
        weight_grad[2],
    )


def solution(mesh):
    data = mesh.shape["dp"]
    cut = Mesh(mesh.devices.reshape(data, HI, LO), ("dp", "hi", "lo"))
    rows = P(("dp", "hi", "lo"), None)
    weight = P(("hi", "lo"), None, None)
    return jax.shard_map(
        body,
        mesh=cut,
        in_specs=(rows, rows, rows, rows, weight, weight, weight),
        out_specs=(rows, rows, rows, weight, weight, weight),
        check_vma=False,
    )
```

time: 434 us -> 253 us (0.58)
  waiting for transfers between devices: 301 us -> 86.4 us
  blocking collectives: 0 us -> 95.9 us
  Pallas kernels: 0 us -> 47.7 us
  other arithmetic: 33.6 us -> 0.26 us
  starting transfers between devices: 37.3 us -> 7.27 us
  local copies, waits for them, and re-layouts: 25.4 us -> 1.31 us
  matrix products: 19.7 us -> 0 us
    all_to_all x4 -> x2, waiting for transfers between devices: 217 us -> 12.1 us  [the longest x1 6.46 us: body(): eo = exchange(expert_out)]
    all_to_all x0 -> x4, blocking collectives: none -> 95.9 us  [the longest x1 26 us: body(): share = over_dp(weight_part).reshape(data, -1, WIDTH).astype(F32)]
    psum x1 -> x0, waiting for transfers between devices: 84.3 us -> none  [body(): totals = lax.psum((grad_gate_part, grad_up_part, grad_down_part), 'dp')]
    all_gather x0 -> x1, waiting for transfers between devices: none -> 70.7 us  [body(): got = lax.all_gather(packed, 'hi', axis=0, tiled=True)]
    pallas_call x0 -> x7, Pallas kernels: none -> 47.7 us  [call(): pl.pallas_call(kernel, out_shape=shapes, in_specs=[SMEM] * scalars + [VME...]
    all_to_all x4 -> x2, starting transfers between devices: 37 us -> 7.19 us  [the longest x1 3.62 us: body(): eo = exchange(expert_out)]
    dot_general x9 -> x0, matrix products: 19.7 us -> none  [the longest x1 3.82 us: body(): jnp.einsum('sech,secl->ehl', by_expert(hidden), grad_in, preferred_elemen...]
    another operation x3 -> x0, other arithmetic: 18.2 us -> none
  transfers between devices with their start and end apart: 5 -> 4, of which waited for: 4 -> 4; matrix products, arithmetic and copies ran while one was open for 8% -> 1% of each run, Pallas kernels for 0% -> 10%
where the time goes in v1:
time: 253 us
  blocking collectives  95.9 us (38%)
  waiting for transfers between devices  86.4 us (34%)
  Pallas kernels  47.7 us (19%)
  between operations  14.1 us (6%)
  starting transfers between devices  7.27 us (3%)
    all_gather x1, waiting for transfers between devices, body(): got = lax.all_gather(packed, 'hi', axis=0, tiled=True)  70.7 us
    pallas_call x7, Pallas kernels, call(): pl.pallas_call(kernel, out_shape=shapes, in_specs=[SMEM] * scalars + [VME...  47.7 us
    all_to_all x1, blocking collectives, body(): share = over_dp(weight_part).reshape(data, -1, WIDTH).astype(F32)  26 us
    all_to_all x1, blocking collectives, body(): over_dp(jnp.tile(share, (data, 1))).reshape(3, 1, WIDTH, WIDTH)  24.2 us
    all_to_all x1, blocking collectives, body(): ib = exchange(input_back)  23 us
    all_to_all x1, blocking collectives, body(): x = exchange(rows_in)  22.6 us
    all_to_all x1, waiting for transfers between devices, body(): eo = exchange(expert_out)  6.46 us
    all_to_all x1, waiting for transfers between devices, body(): og = exchange(out_grad)  5.63 us
  transfers between devices with their start and end apart: 4, of which 4 were waited for; matrix products, arithmetic and copies ran while one was open for 1% of the time, Pallas kernels for 10%

profile of v1, /device:TPU:6, one launch (start us, length us, event | category | flops | bytes accessed | tf_op | source)
XLA Modules:
  0.0 252.9 jit_solution(16513679676187056399)
XLA Ops:
  7.2 0.0 all-gather.2.cloned.1.call-start
  7.2 1.8 shard_map.118
  9.0 0.0 all-gather.2.cloned.1.call-update
  9.0 70.7 %all-gather.2.cloned.1.call-done.got = bf16[8448,128]{1,0:T(8,128)(2,1)} async-done(((bf16[1056,128]{1,0:T(8,128)(2,1)}), bf16[8448,128]{1,0:T(8,128)(2,1)}) %all-gather.2.cloned.1.call-update) | async-done | bytes 2162704 | tf_op jit(solution)/shard_map/all_gather | solution.py:229
  79.7 8.7 %shard_map.119 = (bf16[1280,512]{1,0:T(8,128)(2,1)}, bf16[1280,512]{1,0:T(8,128)(2,1)}, f32[16,512]{1,0:T(8,128)}, f32[16,512]{1,0:T(8,128)}) custom-call(s32[1]{0:T(128)} %bitcast.first, bf16[8448,128]{1,0:T(8,128)(2,1)} %all-gather.2.cloned.1.call-done.got), custom_call_target="tpu_custom_call" | custom-call | flops 1342177280 | bytes 4849668 | tf_op jit(solution)/shard_map/pallas_call | solution.py:46
  88.4 22.6 %all_to_all.62 = bf16[8,160,512]{2,1,0:T(8,128)(2,1)} all-to-all(bf16[8,160,512]{2,1,0:T(8,128)(2,1)} %bitcast.33), channel_id=1, replica_groups=mesh['dp'=8,'hi'=8,'lo'=8] {'lo'}, dimensions={0} | all-to-all | bytes 2621440 | tf_op jit(solution)/shard_map/all_to_all | solution.py:246
  111.0 3.6 %all-to-all-start.2 = ((bf16[8,160,512]{2,1,0:T(8,128)(2,1)}), bf16[8,160,512]{2,1,0:T(8,128)(2,1)S(1)}, u32[]{:S(2)}, u32[]{:S(2)}) async-start(bf16[8,160,512]{2,1,0:T(8,128)(2,1)} %bitcast.10), calls=%async_computation.2 | async-start | bytes 2621440 | tf_op jit(solution)/shard_map/all_to_all | solution.py:247
  114.6 9.1 %shard_map.120 = (bf16[1280,512]{1,0:T(8,128)(2,1)}, bf16[1280,512]{1,0:T(8,128)(2,1)}, f32[1280,512]{1,0:T(8,128)}, f32[1280,512]{1,0:T(8,128)}) custom-call(bf16[1280,512]{1,0:T(8,128)(2,1)} %bitcast.27, bf16[512,512]{1,0:T(8,128)(2,1)} %bitcast.34, bf16[512,512]{1,0:T(8,128)(2,1)} %bitcast.36, bf16[512,512]{1,0:T(8,128)(2,1)} %bitcast.38), custom_call_target="tpu_custom_call" | custom-call | flops 2013265920 | bytes 10747904 | tf_op jit(solution)/shard_map/pallas_call | solution.py:46
  123.6 5.6 %all-to-all-done.2 = bf16[8,160,512]{2,1,0:T(8,128)(2,1)S(1)} async-done(((bf16[8,160,512]{2,1,0:T(8,128)(2,1)}), bf16[8,160,512]{2,1,0:T(8,128)(2,1)S(1)}, u32[]{:S(2)}, u32[]{:S(2)}) %all-to-all-start.2) | async-done | bytes 1310752 | tf_op jit(solution)/shard_map/all_to_all | solution.py:247
  129.3 3.6 %all-to-all-start.1 = ((bf16[8,160,512]{2,1,0:T(8,128)(2,1)}), bf16[8,160,512]{2,1,0:T(8,128)(2,1)S(1)}, u32[]{:S(2)}, u32[]{:S(2)}) async-start(bf16[8,160,512]{2,1,0:T(8,128)(2,1)} %bitcast.30), calls=%async_computation.1 | async-start | bytes 2621440 | tf_op jit(solution)/shard_map/all_to_all | solution.py:256
  132.9 0.0 reduce-scatter.2.cloned.1.call-start
  133.0 10.6 %shard_map.121 = (bf16[1280,512]{1,0:T(8,128)(2,1)}, bf16[1280,512]{1,0:T(8,128)(2,1)}, bf16[1280,512]{1,0:T(8,128)(2,1)}) custom-call(bf16[1280,512]{1,0:T(8,128)(2,1)} %bitcast.23, f32[1280,512]{1,0:T(8,128)} %get-tuple-element.25.act, f32[1280,512]{1,0:T(8,128)} %get-tuple-element.26.slope, bf16[512,512]{1,0:T(8,128)(2,1)} %bitcast.35, ...), custom_call_target="tpu_custom_call" | custom-call | flops 2013265920 | bytes 12058624 | tf_op jit(solution)/shard_map/pallas_call | solution.py:46
  143.5 6.5 %all-to-all-done.1 = bf16[8,160,512]{2,1,0:T(8,128)(2,1)S(1)} async-done(((bf16[8,160,512]{2,1,0:T(8,128)(2,1)}), bf16[8,160,512]{2,1,0:T(8,128)(2,1)S(1)}, u32[]{:S(2)}, u32[]{:S(2)}) %all-to-all-start.1) | async-done | bytes 1310752 | tf_op jit(solution)/shard_map/all_to_all | solution.py:256
  150.0 23.0 %all_to_all.63 = bf16[8,160,512]{2,1,0:T(8,128)(2,1)} all-to-all(bf16[8,160,512]{2,1,0:T(8,128)(2,1)} %bitcast.31), channel_id=1, replica_groups=mesh['dp'=8,'hi'=8,'lo'=8] {'lo'}, dimensions={0} | all-to-all | bytes 2621440 | tf_op jit(solution)/shard_map/all_to_all | solution.py:263
  173.0 9.6 %shard_map.122 = bf16[8320,128]{1,0:T(8,128)(2,1)} custom-call(s32[1]{0:T(128)} %bitcast.first, bf16[8448,128]{1,0:T(8,128)(2,1)} %all-gather.2.cloned.1.call-done.got, f32[16,512]{1,0:T(8,128)} %get-tuple-element.20.rank, f32[16,512]{1,0:T(8,128)} %get-tuple-element.21.gate, bf16[1280,512]{1,0:T(8,128)(2,1)} %bitcast.29, bf16[1280,512]{1,0:T(8,128)(2,1)} %bitcast.32), custom_call_target="tpu_custom_call" | custom-call | flops 2684354560 | bytes 6979588 | tf_op jit(solution)/shard_map/pallas_call | solution.py:46
  182.6 0.0 reduce-scatter.2.cloned.1.call-update
  182.6 6.3 %shard_map.124 = bf16[1536,512]{1,0:T(8,128)(2,1)} custom-call(bf16[1280,512]{1,0:T(8,128)(2,1)} %bitcast.28, bf16[1280,512]{1,0:T(8,128)(2,1)} %bitcast.24, bf16[1280,512]{1,0:T(8,128)(2,1)} %get-tuple-element.31.hidden, bf16[1280,512]{1,0:T(8,128)(2,1)} %get-tuple-element.32.gate_back, bf16[1280,512]{1,0:T(8,128)(2,1)} %get-tuple-element.33.up_back), custom_call_target="tpu_custom_call" | custom-call | flops 2013265920 | bytes 8126464 | tf_op jit(solution)/shard_map/pallas_call | solution.py:46
  188.9 26.0 %all_to_all.64 = bf16[8,192,512]{2,1,0:T(8,128)(2,1)S(1)} all-to-all(bf16[8,192,512]{2,1,0:T(8,128)(2,1)} %bitcast.26), channel_id=1, replica_groups=mesh['dp'=8,'hi'=8,'lo'=8] {'dp'}, dimensions={0} | all-to-all | bytes 3145728 | tf_op jit(solution)/shard_map/all_to_all | solution.py:287
  215.0 0.2 convert_reduce_fusion
  215.2 0.1 tile.2
  215.4 24.2 %all_to_all.65 = bf16[8,192,512]{2,1,0:T(8,128)(2,1)S(1)} all-to-all(bf16[8,192,512]{2,1,0:T(8,128)(2,1)S(1)} %tile.2), channel_id=1, replica_groups=mesh['dp'=8,'hi'=8,'lo'=8] {'dp'}, dimensions={0} | all-to-all | bytes 3145728 | tf_op jit(solution)/shard_map/all_to_all | solution.py:290
  239.6 1.2 slice_bitcast_fusion
  240.8 3.6 %reduce-scatter.2.cloned.1.call-done.got = bf16[1040,128]{1,0:T(8,128)(2,1)} async-done(((bf16[8320,128]{1,0:T(8,128)(2,1)}), bf16[1040,128]{1,0:T(8,128)(2,1)}) %reduce-scatter.2.cloned.1.call-update) | async-done | bytes 266256 | tf_op jit(solution)/shard_map/reduce_scatter | solution.py:282
  244.4 1.7 shard_map.123
  (5 shorter events, 0.0 us)
Async XLA Ops:
  7.2 72.6 %all-gather.2.cloned.1.call-start = ((), (), s32[]{:S(2)}) async-start(), calls=%async_computation.7 | async-start | bytes 2433024 | tf_op jit(solution)/shard_map/all_gather | solution.py:229
  111.0 18.3 %all-to-all-start.2 = ((bf16[8,160,512]{2,1,0:T(8,128)(2,1)}), bf16[8,160,512]{2,1,0:T(8,128)(2,1)S(1)}, u32[]{:S(2)}, u32[]{:S(2)}) async-start(bf16[8,160,512]{2,1,0:T(8,128)(2,1)} %bitcast.10), calls=%async_computation.2 | async-start | bytes 2621440 | tf_op jit(solution)/shard_map/all_to_all | solution.py:247
  129.3 3.7 %copy-start = (bf16[8,160,512]{2,1,0:T(8,128)(2,1)}, bf16[8,160,512]{2,1,0:T(8,128)(2,1)S(1)}, u32[]{:S(2)}) copy-start(bf16[8,160,512]{2,1,0:T(8,128)(2,1)S(1)} %all-to-all-done.2) | copy-start | bytes 3932164
  129.3 20.7 %all-to-all-start.1 = ((bf16[8,160,512]{2,1,0:T(8,128)(2,1)}), bf16[8,160,512]{2,1,0:T(8,128)(2,1)S(1)}, u32[]{:S(2)}, u32[]{:S(2)}) async-start(bf16[8,160,512]{2,1,0:T(8,128)(2,1)} %bitcast.30), calls=%async_computation.1 | async-start | bytes 2621440 | tf_op jit(solution)/shard_map/all_to_all | solution.py:256
  132.9 111.5 %reduce-scatter.2.cloned.1.call-start = ((), (), s32[]{:S(2)}) async-start(), calls=%async_computation.8 | async-start | bytes 2396160 | tf_op jit(solution)/shard_map/reduce_scatter | solution.py:282
  150.0 23.0 %copy-start.1 = (bf16[8,160,512]{2,1,0:T(8,128)(2,1)}, bf16[8,160,512]{2,1,0:T(8,128)(2,1)S(1)}, u32[]{:S(2)}) copy-start(bf16[8,160,512]{2,1,0:T(8,128)(2,1)S(1)} %all-to-all-done.1) | copy-start | bytes 3932164
Sparse Core Ops, SparseCore 0:
  10.7 69.0 all-gather.1
  182.7 61.5 reduce-scatter.1

commit v2 on v1

v2 whole, which is shorter than its diff:
```python
import functools
import jax
import jax.numpy as jnp
from jax import lax
from jax.experimental import pallas as pl
from jax.experimental.pallas import tpu as pltpu
from jax.sharding import Mesh, PartitionSpec as P

BF = jnp.bfloat16
F32 = jnp.float32
TOK = 128
WIDTH = 512
TOP = 8
CAP = 20
HI = 8
LO = 8
PACK = 4
GROUPS = HI // PACK
SLOTS = PACK * CAP
GTOK = PACK * TOK
LANES = 128
CUTS = WIDTH // LANES
FIRST = 3
SECOND = CUTS - FIRST
LEAD = FIRST * LANES
TAIL = SECOND * LANES
SENT_RING = LEAD + 2 * TOP
SENT_REST = TAIL + WIDTH + 4 * TOP
AT_COT = TAIL
AT_GATES = TAIL + WIDTH
BACK = 2 * WIDTH + 2 * TOP
STEPS = [0] + [s for h in range(1, HI // 2) for s in (-h, h)] + [-(HI // 2)]
ALL = LO * SLOTS
ROWS = HI * CAP * LO
MIB = 1024 * 1024
VMEM = pl.BlockSpec(memory_space=pltpu.VMEM)
SMEM = pl.BlockSpec(memory_space=pltpu.SMEM)


def nn(a, b):
    return jnp.dot(a, b, preferred_element_type=F32)


def nt(a, b):
    return lax.dot_general(a, b, (((1,), (1,)), ((), ())), preferred_element_type=F32)


def tn(a, b):
    return lax.dot_general(a, b, (((0,), (0,)), ((), ())), preferred_element_type=F32)


def call(kernel, shapes, args, scratch=(), scalars=0, flops=0, room=24):
    moved = sum(a.size * a.dtype.itemsize for a in args)
    moved += sum(s.size * s.dtype.itemsize for s in shapes)
    return pl.pallas_call(
        kernel,
        out_shape=shapes,
        in_specs=[SMEM] * scalars + [VMEM] * (len(args) - scalars),
        out_specs=[VMEM] * len(shapes),
        scratch_shapes=list(scratch),
        compiler_params=pltpu.CompilerParams(vmem_limit_bytes=room * MIB),
        cost_estimate=pl.CostEstimate(flops=flops, bytes_accessed=moved, transcendentals=0),
    )(*args)


def pack_kernel(tok, ids, gates, cot, ring_out, rest_out):
    for f in range(CUTS):
        cut = slice(f * LANES, (f + 1) * LANES)
        to, at = (ring_out, f) if f < FIRST else (rest_out, f - FIRST)
        to[at * TOK : (at + 1) * TOK, :] = tok[:, cut]
        rest_out[AT_COT + f * TOK : AT_COT + (f + 1) * TOK, :] = cot[:, cut]
    gate = gates[...]
    high = gate.astype(BF).astype(F32)
    middle = (gate - high).astype(BF).astype(F32)
    low = gate - high - middle
    named = ids[...].astype(F32)
    ring_out[LEAD : LEAD + 16, :] = jnp.concatenate([named, named], axis=0).astype(BF)
    rest_out[AT_GATES : AT_GATES + 16, :] = jnp.concatenate([high, middle], axis=0).astype(BF)
    rest_out[AT_GATES + 16 : AT_GATES + 32, :] = jnp.concatenate([low, low], axis=0).astype(BF)


def upper(size):
    row = lax.broadcasted_iota(jnp.int32, (size, size), 0)
    col = lax.broadcasted_iota(jnp.int32, (size, size), 1)
    return (row <= col).astype(F32).astype(BF)


def place_rows():
    return (lax.broadcasted_iota(jnp.int32, (SLOTS, GTOK), 0) + 1).astype(F32)


def pick_rows(rank, group, pick_s):
    place = place_rows()
    for e in range(LO):
        picks = rank[group * LO + e : group * LO + e + 1, :] == place
        pick_s[e * SLOTS : (e + 1) * SLOTS, :] = jnp.where(picks, 1.0, 0.0).astype(BF)


def put_rows(out, group, rows, lanes):
    for e in range(LO):
        to = (e * GROUPS + group) * SLOTS
        out[to : to + SLOTS, lanes] = rows[e * SLOTS : (e + 1) * SLOTS, :].astype(BF)


def first_kernel(first, *refs):
    blocks, (x_out, rank_out, ids_out, tok_s, pick_s) = refs[:HI], refs[HI:]
    base = (first[0] * LO).astype(F32)
    upto = upper(GTOK)
    for g in range(GROUPS):
        part = []
        for b in range(PACK):
            got = blocks[g * PACK + b]
            for f in range(FIRST):
                cut = slice(f * LANES, (f + 1) * LANES)
                tok_s[b * TOK : (b + 1) * TOK, cut] = got[f * TOK : (f + 1) * TOK, :]
            part.append(got[LEAD : LEAD + 16, :].astype(F32)[:TOP])
        ids = jnp.concatenate(part, axis=1)
        ids_out[g * TOP : (g + 1) * TOP, :] = ids
        named = [
            jnp.sum(jnp.where(ids == base + e, 1.0, 0.0), axis=0, keepdims=True)
            for e in range(LO)
        ]
        named = jnp.concatenate(named, axis=0)
        rank_out[g * LO : (g + 1) * LO, :] = named * nn(named.astype(BF), upto)
        pick_rows(rank_out, g, pick_s)
        put_rows(x_out, g, nn(pick_s[...], tok_s[...]), slice(0, LEAD))


def source(first, step):
    return lax.rem(first[0] + step + HI, HI)


def rest_group(first, got, group, begin, count, kept):
    for b in range(PACK):
        at = source(first, STEPS[group * PACK + b]) * SENT_REST + begin
        for f in range(count):
            here = pl.ds(pl.multiple_of(at + f * TOK, 16), TOK)
            kept[b * TOK : (b + 1) * TOK, f * LANES : (f + 1) * LANES] = got[here, :]


def rest_kernel(first, got, rank, ids, out, gate_out, tok_s, cot_s, pick_s):
    base = (first[0] * LO).astype(F32)
    for g in range(GROUPS):
        rest_group(first, got, g, 0, SECOND, tok_s)
        rest_group(first, got, g, AT_COT, CUTS, cot_s)
        part = []
        for b in range(PACK):
            at = source(first, STEPS[g * PACK + b]) * SENT_REST + AT_GATES
            one = got[pl.ds(pl.multiple_of(at, 16), 16), :].astype(F32)
            two = got[pl.ds(pl.multiple_of(at + 16, 16), 16), :].astype(F32)
            part.append((one[:TOP] + one[TOP:]) + two[:TOP])
        gates = jnp.concatenate(part, axis=1)
        named = ids[g * TOP : (g + 1) * TOP, :]
        weight = [
            jnp.sum(jnp.where(named == base + e, gates, 0.0), axis=0, keepdims=True)
            for e in range(LO)
        ]
        gate_out[g * LO : (g + 1) * LO, :] = jnp.concatenate(weight, axis=0)
        pick_rows(rank, g, pick_s)
        scale = []
        for e in range(LO):
            picked = pick_s[e * SLOTS : (e + 1) * SLOTS, :].astype(F32)
            scale.append(jnp.sum(picked * weight[e], axis=1, keepdims=True))
        put_rows(out, g, nn(pick_s[...], tok_s[...]), slice(0, TAIL))
        grads = jnp.concatenate(scale, axis=0) * nn(pick_s[...], cot_s[...])
        put_rows(out, g, grads, slice(TAIL, TAIL + WIDTH))


TILE = 160


def tiles(step):
    def one(i, carry):
        step(pl.ds(pl.multiple_of(i * TILE, 16), TILE))
        return carry

    lax.fori_loop(0, ROWS // TILE, one, 0)


def gated(x, rest, w_gate, w_up, rows):
    tok = jnp.concatenate([x[rows, :], rest[rows, :TAIL]], axis=1)
    gate_pre = nn(tok, w_gate[...])
    up_pre = nn(tok, w_up[...])
    sig = jax.nn.sigmoid(gate_pre)
    activation = gate_pre * sig
    hidden = (activation * up_pre).astype(BF)
    return gate_pre, up_pre, sig, activation, hidden


def forward_kernel(x, rest, w_gate, w_up, w_down, out):
    def step(rows):
        hidden = gated(x, rest, w_gate, w_up, rows)[-1]
        out[rows, :] = nn(hidden, w_down[...]).astype(BF)

    tiles(step)


def backward_kernel(x, rest, w_gate, w_up, w_down, out, weight, hidden_s, gate_s, up_s):
    def step(rows):
        gate_pre, up_pre, sig, activation, hidden = gated(x, rest, w_gate, w_up, rows)
        hidden_grad = nt(rest[rows, TAIL:], w_down[...])
        slope = sig * (1.0 + gate_pre * (1.0 - sig))
        gate = (hidden_grad * up_pre * slope).astype(BF)
        up = (hidden_grad * activation).astype(BF)
        hidden_s[rows, :] = hidden
        gate_s[rows, :] = gate
        up_s[rows, :] = up
        out[rows, :] = (nt(gate, w_gate[...]) + nt(up, w_up[...])).astype(BF)

    tiles(step)
    for n, side in enumerate((gate_s, up_s)):
        at = n * WIDTH
        weight[at : at + LEAD, :] = tn(x[...], side[...]).astype(BF)
        weight[at + LEAD : at + WIDTH, :] = tn(rest[:, :TAIL], side[...]).astype(BF)
    weight[2 * WIDTH : 3 * WIDTH, :] = tn(hidden_s[...], rest[:, TAIL:]).astype(BF)


def split(value):
    high = value.astype(BF)
    return high, (value - high.astype(F32)).astype(BF)


def layer_kernel(first, got, rank, ids, gate, eo, out, picks_out, cot_s, eo_s):
    base = (first[0] * LO).astype(F32)
    expert = lax.broadcasted_iota(jnp.int32, (LO, ALL), 0)
    slot = lax.broadcasted_iota(jnp.int32, (LO, ALL), 1)
    spread = ((slot >= expert * SLOTS) & (slot < (expert + 1) * SLOTS)).astype(F32).astype(BF)
    lane = lax.broadcasted_iota(jnp.int32, (1, ALL), 1)
    place = (lane - SLOTS * lax.div(lane, SLOTS) + 1).astype(F32)
    for g in range(GROUPS):
        rest_group(first, got, g, AT_COT, CUTS, cot_s)
        for e in range(LO):
            at = (e * GROUPS + g) * SLOTS
            eo_s[e * SLOTS : (e + 1) * SLOTS, :] = eo[at : at + SLOTS, :]
        rows = slice(g * LO, (g + 1) * LO)
        picks = tn(rank[rows, :].astype(BF), spread) == place
        picks_out[g * GTOK : (g + 1) * GTOK, :] = jnp.where(picks, 1.0, 0.0).astype(BF)
        high, low = split(gate[rows, :])
        high = jnp.where(picks, tn(high, spread), 0.0).astype(BF)
        low = jnp.where(picks, tn(low, spread), 0.0).astype(BF)
        layer = nn(high, eo_s[...]) + nn(low, eo_s[...])
        along = jnp.where(picks, nt(cot_s[...], eo_s[...]), 0.0)
        high, low = split(along)
        along = nt(spread, high) + nt(spread, low)
        named = ids[g * TOP : (g + 1) * TOP, :]
        grad = jnp.zeros((TOP, GTOK), F32)
        for e in range(LO):
            grad += jnp.where(named == base + e, along[e : e + 1, :], 0.0)
        grad_high = grad.astype(BF).astype(F32)
        grad = jnp.concatenate([grad_high, grad - grad_high], axis=0).astype(BF)
        for b in range(PACK):
            at = source(first, STEPS[g * PACK + b])
            for f in range(CUTS):
                here = layer[b * TOK : (b + 1) * TOK, f * LANES : (f + 1) * LANES]
                out[at, f * TOK : (f + 1) * TOK, :] = here.astype(BF)
            out[at, 2 * WIDTH : BACK, :] = grad[:, b * TOK : (b + 1) * TOK]


def back_kernel(first, picks, ib, held, out, ib_s, sent_s, sems):
    del held
    copies = []
    for g in range(GROUPS):
        for e in range(LO):
            at = (e * GROUPS + g) * SLOTS
            ib_s[e * SLOTS : (e + 1) * SLOTS, :] = ib[at : at + SLOTS, :]
        back = nn(picks[g * GTOK : (g + 1) * GTOK, :], ib_s[...])
        for b in range(PACK):
            n = g * PACK + b
            for f in range(CUTS):
                here = back[b * TOK : (b + 1) * TOK, f * LANES : (f + 1) * LANES]
                sent_s[n, f * TOK : (f + 1) * TOK, :] = here.astype(BF)
            copy = pltpu.make_async_copy(
                sent_s.at[n],
                out.at[source(first, STEPS[n]), pl.ds(WIDTH, WIDTH), :],
                sems.at[n],
            )
            copy.start()
            copies.append(copy)
    for copy in copies:
        copy.wait()


def unpack_kernel(got, layer, back, grad):
    for f in range(CUTS):
        cut = slice(f * LANES, (f + 1) * LANES)
        layer[:, cut] = got[f * TOK : (f + 1) * TOK, :]
        back[:, cut] = got[WIDTH + f * TOK : WIDTH + (f + 1) * TOK, :]
    parts = got[2 * WIDTH : BACK, :].astype(F32)
    grad[...] = parts[:TOP] + parts[TOP:]


def body(tokens, expert_ids, gate_weights, cotangent, w_gate, w_up, w_down):
    shape = jax.ShapeDtypeStruct
    first = lax.axis_index("hi").astype(jnp.int32).reshape(1)
    w_gate, w_up, w_down = w_gate[0], w_up[0], w_down[0]
    square = 2 * ROWS * WIDTH * WIDTH
    ring_sent, rest_sent = call(
        pack_kernel,
        [shape((SENT_RING, LANES), BF), shape((SENT_REST, LANES), BF)],
        [tokens, expert_ids.T, gate_weights.T, cotangent],
        room=56,
    )
    got = lax.all_gather(rest_sent, "hi", axis=0, tiled=True)
    after = [(i, (i + 1) % HI) for i in range(HI)]
    before = [(i, (i - 1) % HI) for i in range(HI)]
    blocks = {0: ring_sent}
    for h in range(1, HI // 2 + 1):
        blocks[-h] = lax.ppermute(blocks[1 - h], "hi", after)
        if h < HI // 2:
            blocks[h] = lax.ppermute(blocks[h - 1], "hi", before)
    picked = pltpu.VMEM((ALL, GTOK), BF)
    rows_first, rank, ids = call(
        first_kernel,
        [
            shape((ROWS, LEAD), BF),
            shape((GROUPS * LO, GTOK), F32),
            shape((GROUPS * TOP, GTOK), F32),
        ],
        [first] + [blocks[s] for s in STEPS],
        [pltpu.VMEM((GTOK, LEAD), BF), picked],
        scalars=1,
    )
    rows_rest, gate = call(
        rest_kernel,
        [shape((ROWS, TAIL + WIDTH), BF), shape((GROUPS * LO, GTOK), F32)],
        [first, got, rank, ids],
        [pltpu.VMEM((GTOK, TAIL), BF), pltpu.VMEM((GTOK, WIDTH), BF), picked],
        scalars=1,
        flops=100 * square,
    )
    exchange = functools.partial(
        lax.all_to_all, axis_name="lo", split_axis=0, concat_axis=0, tiled=True
    )
    x = exchange(rows_first)
    rest = exchange(rows_rest)
    narrow = shape((ROWS, WIDTH), BF)
    (expert_out,) = call(
        forward_kernel, [narrow], [x, rest, w_gate, w_up, w_down], flops=3 * square
    )
    eo = exchange(expert_out)
    whole = pltpu.VMEM((ROWS, WIDTH), BF)
    input_back, weight_part = call(
        backward_kernel,
        [narrow, shape((3 * WIDTH, WIDTH), BF)],
        [x, rest, w_gate, w_up, w_down],
        [whole, whole, whole],
        flops=8 * square,
    )
    eo, input_back = lax.optimization_barrier((eo, input_back))
    ib = exchange(input_back)
    partial, picks = call(
        layer_kernel,
        [shape((HI, BACK, LANES), BF), shape((GROUPS * GTOK, ALL), BF)],
        [first, got, rank, ids, gate, eo],
        [pltpu.VMEM((GTOK, WIDTH), BF), pltpu.VMEM((ALL, WIDTH), BF)],
        scalars=1,
        flops=3 * square,
    )
    partial = pl.pallas_call(
        back_kernel,
        out_shape=shape((HI, BACK, LANES), BF),
        in_specs=[SMEM, VMEM, VMEM, pl.BlockSpec(memory_space=pl.ANY)],
        out_specs=pl.BlockSpec(memory_space=pl.ANY),
        scratch_shapes=[
            pltpu.VMEM((ALL, WIDTH), BF),
            pltpu.VMEM((HI, WIDTH, LANES), BF),
            pltpu.SemaphoreType.DMA((HI,)),
        ],
        input_output_aliases={3: 0},
        compiler_params=pltpu.CompilerParams(vmem_limit_bytes=24 * MIB),
        cost_estimate=pl.CostEstimate(flops=square, bytes_accessed=4 << 20, transcendentals=0),
    )(first, picks, ib, partial)
    summed = lax.psum_scatter(
        partial.reshape(HI * BACK, LANES), "hi", scatter_dimension=0, tiled=True
    )
    over_dp = functools.partial(
        lax.all_to_all, axis_name="dp", split_axis=0, concat_axis=0, tiled=True
    )
    data = lax.axis_size("dp")
    share = over_dp(weight_part).reshape(data, -1, WIDTH).astype(F32)
    grad_scale = float(data * TOK * TOP) ** (-0.5)
    share = (jnp.sum(share, axis=0) * grad_scale).astype(BF)
    weight_grad = over_dp(jnp.tile(share, (data, 1))).reshape(3, 1, WIDTH, WIDTH)
    layer_out, grad_tokens, grad_gates = call(
        unpack_kernel,
        [shape((TOK, WIDTH), BF), shape((TOK, WIDTH), BF), shape((TOP, LANES), F32)],
        [summed],
        room=56,
    )
    return (
        layer_out,
        grad_tokens,
        grad_gates.T,
        weight_grad[0],
        weight_grad[1],
        weight_grad[2],
    )


def solution(mesh):
    data = mesh.shape["dp"]
    cut = Mesh(mesh.devices.reshape(data, HI, LO), ("dp", "hi", "lo"))
    rows = P(("dp", "hi", "lo"), None)
    weight = P(("hi", "lo"), None, None)
    return jax.shard_map(
        body,
        mesh=cut,
        in_specs=(rows, rows, rows, rows, weight, weight, weight),
        out_specs=(rows, rows, rows, weight, weight, weight),
        check_vma=False,
    )
```

time: 253 us -> 230 us (0.909)
  waiting for transfers between devices: 86.4 us -> 42.6 us
  starting transfers between devices: 7.27 us -> 50.7 us
  blocking collectives: 95.9 us -> 75.3 us
  Pallas kernels: 47.7 us -> 31.8 us
  local copies, waits for them, and re-layouts: 1.31 us -> 13.6 us
    all_gather x1, waiting for transfers between devices: 70.7 us -> 8.21 us  [body(): got = lax.all_gather(rest_sent, 'hi', axis=0, tiled=True)]
    ppermute x0 -> x7, starting transfers between devices: none -> 33.3 us  [the longest x3 22.3 us: body(): blocks[h] = lax.ppermute(blocks[h - 1], 'hi', before)]
    all_to_all x2 -> x1, blocking collectives: 45.6 us -> 26.9 us  [body(): rest = exchange(rows_rest)]
    pallas_call x7, Pallas kernels: 47.7 us -> 30 us  [call(): pl.pallas_call(kernel, out_shape=shapes, in_specs=[SMEM] * scalars + [VME...]
    ppermute x0 -> x7, waiting for transfers between devices: none -> 16.2 us  [the longest x4 9.28 us: body(): blocks[-h] = lax.ppermute(blocks[1 - h], 'hi', after)]
    unnamed x4 -> x30, local copies, waits for them, and re-layouts: 0.01 us -> 12.3 us
    all_to_all x1 -> x2, starting transfers between devices: 3.57 us -> 13.1 us  [the longest x1 8.59 us: body(): x = exchange(rows_first)]
    all_to_all x1, waiting for transfers between devices: 6.46 us -> 1.14 us  [body(): eo = exchange(expert_out)]
  transfers between devices with their start and end apart: 4 -> 12, of which waited for: 4 -> 12; matrix products, arithmetic and copies ran while one was open for 1% -> 1% of each run, Pallas kernels for 10% -> 9%
where the time goes in v2:
time: 230 us; the launch traced here: 228 us
  blocking collectives  75.3 us (33%)
  starting transfers between devices  50.7 us (22%)
  waiting for transfers between devices  42.6 us (19%)
  Pallas kernels  31.8 us (14%)
  between operations  14.2 us (6%)
  local copies, waits for them, and re-layouts  13.6 us (6%)
    pallas_call x7, Pallas kernels, call(): pl.pallas_call(kernel, out_shape=shapes, in_specs=[SMEM] * scalars + [VME...  30 us
    all_to_all x1, blocking collectives, body(): rest = exchange(rows_rest)  26.9 us
    all_to_all x1, blocking collectives, body(): over_dp(jnp.tile(share, (data, 1))).reshape(3, 1, WIDTH, WIDTH)  24.2 us
    all_to_all x1, blocking collectives, body(): share = over_dp(weight_part).reshape(data, -1, WIDTH).astype(F32)  24.2 us
    ppermute x3, starting transfers between devices, body(): blocks[h] = lax.ppermute(blocks[h - 1], 'hi', before)  22.3 us
    unnamed x30, local copies, waits for them, and re-layouts  12.3 us
    ppermute x4, starting transfers between devices, body(): blocks[-h] = lax.ppermute(blocks[1 - h], 'hi', after)  11 us
    ppermute x4, waiting for transfers between devices, body(): blocks[-h] = lax.ppermute(blocks[1 - h], 'hi', after)  9.28 us
  transfers between devices with their start and end apart: 12, of which 12 were waited for; matrix products, arithmetic and copies ran while one was open for 1% of the time, Pallas kernels for 9%

profile of v2, /device:TPU:6, one launch (start us, length us, event | category | flops | bytes accessed | tf_op | source)
XLA Modules:
  0.0 228.4 jit_solution(836303602414250818)
XLA Ops:
  9.0 5.2 %collective-permute-start = (bf16[400,128]{1,0:T(8,128)(2,1)}, bf16[400,128]{1,0:T(8,128)(2,1)S(1)}, u32[]{:S(2)}, u32[]{:S(2)}) collective-permute-start(bf16[400,128]{1,0:T(8,128)(2,1)} %get-tuple-element.23.refs_0_), channel_id=1, source_target_pairs={{0,8},{8,16},{16,24},{24,32},{32,40},{40,48},{48,56},{56,0},{1,9},... | collective-permute-start | bytes 307208 | tf_op jit(solution)/shard_map/ppermute | solution.py:308
  14.2 8.6 %collective-permute-start.1 = (bf16[400,128]{1,0:T(8,128)(2,1)}, bf16[400,128]{1,0:T(8,128)(2,1)S(1)}, u32[]{:S(2)}, u32[]{:S(2)}) collective-permute-start(bf16[400,128]{1,0:T(8,128)(2,1)} %get-tuple-element.23.refs_0_), channel_id=1, source_target_pairs={{0,56},{8,0},{16,8},{24,16},{32,24},{40,32},{48,40},{56,48},{1,57}... | collective-permute-start | bytes 307208 | tf_op jit(solution)/shard_map/ppermute | solution.py:310
  24.5 1.9 collective-permute-start.2
  27.4 6.3 %collective-permute-start.3 = (bf16[400,128]{1,0:T(8,128)(2,1)S(1)}, bf16[400,128]{1,0:T(8,128)(2,1)S(1)}, u32[]{:S(2)}, u32[]{:S(2)}) collective-permute-start(bf16[400,128]{1,0:T(8,128)(2,1)S(1)} %collective-permute-done.1.refs_2_), channel_id=1, source_target_pairs={{0,56},{8,0},{16,8},{24,16},{32,24},{40,32},{48,40},{56,48},{1,57}... | collective-permute-start | bytes 307208 | tf_op jit(solution)/shard_map/ppermute | solution.py:310
  34.0 2.0 collective-permute-start.4
  35.9 2.4 %collective-permute-done.3.refs_4_ = bf16[400,128]{1,0:T(8,128)(2,1)S(1)} collective-permute-done((bf16[400,128]{1,0:T(8,128)(2,1)S(1)}, bf16[400,128]{1,0:T(8,128)(2,1)S(1)}, u32[]{:S(2)}, u32[]{:S(2)}) %collective-permute-start.3) | collective-permute-done | bytes 102432 | tf_op jit(solution)/shard_map/ppermute | solution.py:310
  38.3 7.4 %collective-permute-start.5 = (bf16[400,128]{1,0:T(8,128)(2,1)S(1)}, bf16[400,128]{1,0:T(8,128)(2,1)S(1)}, u32[]{:S(2)}, u32[]{:S(2)}) collective-permute-start(bf16[400,128]{1,0:T(8,128)(2,1)S(1)} %collective-permute-done.3.refs_4_), channel_id=1, source_target_pairs={{0,56},{8,0},{16,8},{24,16},{32,24},{40,32},{48,40},{56,48},{1,57}... | collective-permute-start | bytes 307208 | tf_op jit(solution)/shard_map/ppermute | solution.py:310
  45.7 2.9 %collective-permute-done.4.refs_5_ = bf16[400,128]{1,0:T(8,128)(2,1)S(1)} collective-permute-done((bf16[400,128]{1,0:T(8,128)(2,1)S(1)}, bf16[400,128]{1,0:T(8,128)(2,1)S(1)}, u32[]{:S(2)}, u32[]{:S(2)}) %collective-permute-start.4) | collective-permute-done | bytes 102432 | tf_op jit(solution)/shard_map/ppermute | solution.py:308
  50.5 3.5 %collective-permute-done.5.refs_6_ = bf16[400,128]{1,0:T(8,128)(2,1)S(1)} collective-permute-done((bf16[400,128]{1,0:T(8,128)(2,1)S(1)}, bf16[400,128]{1,0:T(8,128)(2,1)S(1)}, u32[]{:S(2)}, u32[]{:S(2)}) %collective-permute-start.5) | collective-permute-done | bytes 102432 | tf_op jit(solution)/shard_map/ppermute | solution.py:310
  54.0 4.5 %collective-permute-done.6.refs_7_ = bf16[400,128]{1,0:T(8,128)(2,1)S(1)} collective-permute-done((bf16[400,128]{1,0:T(8,128)(2,1)S(1)}, bf16[400,128]{1,0:T(8,128)(2,1)S(1)}, u32[]{:S(2)}, u32[]{:S(2)}) %collective-permute-start.6) | collective-permute-done | bytes 102432 | tf_op jit(solution)/shard_map/ppermute | solution.py:308
  59.5 2.2 shard_map.119
  61.7 8.6 %all-to-all-start = ((bf16[8,160,384]{2,1,0:T(8,128)(2,1)}), bf16[8,160,384]{2,1,0:T(8,128)(2,1)S(1)}, u32[]{:S(2)}, u32[]{:S(2)}) async-start(bf16[8,160,384]{2,1,0:T(8,128)(2,1)} %bitcast.3), calls=%async_computation | async-start | bytes 1966080 | tf_op jit(solution)/shard_map/all_to_all | solution.py:334
  70.3 8.2 %all-gather.2.cloned.1.call-done.got = bf16[5376,128]{1,0:T(8,128)(2,1)} async-done(((bf16[672,128]{1,0:T(8,128)(2,1)}), bf16[5376,128]{1,0:T(8,128)(2,1)}) %all-gather.2.cloned.1.call-update) | async-done | bytes 1376272 | tf_op jit(solution)/shard_map/all_gather | solution.py:303
  81.4 3.4 %all-to-all-done = bf16[8,160,384]{2,1,0:T(8,128)(2,1)S(1)} async-done(((bf16[8,160,384]{2,1,0:T(8,128)(2,1)}), bf16[8,160,384]{2,1,0:T(8,128)(2,1)S(1)}, u32[]{:S(2)}, u32[]{:S(2)}) %all-to-all-start) | async-done | bytes 983072 | tf_op jit(solution)/shard_map/all_to_all | solution.py:334
  85.8 26.9 %all_to_all.63 = bf16[8,160,640]{2,1,0:T(8,128)(2,1)S(1)} all-to-all(bf16[8,160,640]{2,1,0:T(8,128)(2,1)S(1)} %bitcast.27), channel_id=1, replica_groups=mesh['dp'=8,'hi'=8,'lo'=8] {'lo'}, dimensions={0} | all-to-all | bytes 3276800 | tf_op jit(solution)/shard_map/all_to_all | solution.py:335
  112.6 5.3 %shard_map.121 = bf16[1280,512]{1,0:T(8,128)(2,1)} custom-call(bf16[1280,384]{1,0:T(8,128)(2,1)S(1)} %bitcast.30, bf16[1280,640]{1,0:T(8,128)(2,1)S(1)} %bitcast.25, bf16[512,512]{1,0:T(8,128)(2,1)S(1)} %bitcast.32, bf16[512,512]{1,0:T(8,128)(2,1)S(1)} %bitcast.34, bf16[512,512]{1,0:T(8,128)(2,1)S(1)} %bitcast.36), custom_call_target="tpu_custom_call" | custom-call | flops 2013265920 | bytes 5505024 | tf_op jit(solution)/shard_map/pallas_call | solution.py:55
  118.0 4.3 %all-to-all-start.2 = ((bf16[8,160,512]{2,1,0:T(8,128)(2,1)}), bf16[8,160,512]{2,1,0:T(8,128)(2,1)}, u32[]{:S(2)}, u32[]{:S(2)}) async-start(bf16[8,160,512]{2,1,0:T(8,128)(2,1)} %bitcast.10), calls=%async_computation.2 | async-start | bytes 2621440 | tf_op jit(solution)/shard_map/all_to_all | solution.py:340
  126.6 9.6 %shard_map.122 = (bf16[1280,512]{1,0:T(8,128)(2,1)S(1)}, bf16[1536,512]{1,0:T(8,128)(2,1)S(1)}) custom-call(bf16[1280,384]{1,0:T(8,128)(2,1)S(1)} %bitcast.31, bf16[1280,640]{1,0:T(8,128)(2,1)S(1)} %bitcast.26, bf16[512,512]{1,0:T(8,128)(2,1)S(1)} %bitcast.33, bf16[512,512]{1,0:T(8,128)(2,1)S(1)} %bitcast.35, bf16[512,512]{1,0:T(8,128)(2,1)S(1)} %bitcast.37), custom_call_target="tpu_custom_call" | custom-call | flops 5368709120 | bytes 7077888 | tf_op jit(solution)/shard_map/pallas_call | solution.py:55
  138.4 4.5 %all-to-all-start.3 = ((bf16[8,160,512]{2,1,0:T(8,128)(2,1)}), bf16[8,160,512]{2,1,0:T(8,128)(2,1)S(1)}, u32[]{:S(2)}, u32[]{:S(2)}) async-start(bf16[8,160,512]{2,1,0:T(8,128)(2,1)} %bitcast.29), calls=%async_computation.3 | async-start | bytes 2621440 | tf_op jit(solution)/shard_map/all_to_all | solution.py:350
  144.3 7.8 %shard_map.123 = (bf16[8,1040,128]{2,1,0:T(8,128)(2,1)}, bf16[1024,640]{1,0:T(8,128)(2,1)S(1)}) custom-call(s32[1]{0:T(128)} %bitcast.first, bf16[5376,128]{1,0:T(8,128)(2,1)S(1)} %copy-done.8, f32[16,512]{1,0:T(8,128)S(1)} %get-tuple-element.24.rank, f32[16,512]{1,0:T(8,128)S(1)} %get-tuple-element.25.ids, f32[16,512]{1,0:T(8,128)S(1)} %get-tuple-element.26.gate, ...), custom_call_target="tpu_custom_call" | custom-call | flops 2013265920 | bytes 6225924 | tf_op jit(solution)/shard_map/pallas_call | solution.py:55
  153.1 6.7 %all-to-all-done.3 = bf16[8,160,512]{2,1,0:T(8,128)(2,1)S(1)} async-done(((bf16[8,160,512]{2,1,0:T(8,128)(2,1)}), bf16[8,160,512]{2,1,0:T(8,128)(2,1)S(1)}, u32[]{:S(2)}, u32[]{:S(2)}) %all-to-all-start.3) | async-done | bytes 1310752 | tf_op jit(solution)/shard_map/all_to_all | solution.py:350
  162.9 24.2 %all_to_all.64 = bf16[8,192,512]{2,1,0:T(8,128)(2,1)S(1)} all-to-all(bf16[8,192,512]{2,1,0:T(8,128)(2,1)S(1)} %bitcast.28), channel_id=1, replica_groups=mesh['dp'=8,'hi'=8,'lo'=8] {'dp'}, dimensions={0} | all-to-all | bytes 3145728 | tf_op jit(solution)/shard_map/all_to_all | solution.py:380
  187.6 24.2 %all_to_all.65 = bf16[8,192,512]{2,1,0:T(8,128)(2,1)S(1)} all-to-all(bf16[8,192,512]{2,1,0:T(8,128)(2,1)S(1)} %tile.2), channel_id=1, replica_groups=mesh['dp'=8,'hi'=8,'lo'=8] {'dp'}, dimensions={0} | all-to-all | bytes 3145728 | tf_op jit(solution)/shard_map/all_to_all | solution.py:383
  213.0 6.9 %reduce-scatter.2.cloned.1.call-done.got = bf16[1040,128]{1,0:T(8,128)(2,1)} async-done(((bf16[8320,128]{1,0:T(8,128)(2,1)}), bf16[1040,128]{1,0:T(8,128)(2,1)}) %reduce-scatter.2.cloned.1.call-update) | async-done | bytes 266256 | tf_op jit(solution)/shard_map/reduce_scatter | solution.py:373
  (47 shorter events, 26.6 us)
Async XLA Ops:
  7.2 71.3 %all-gather.2.cloned.1.call-start = ((), (), s32[]{:S(2)}) async-start(), calls=%async_computation.7 | async-start | bytes 1548288 | tf_op jit(solution)/shard_map/all_gather | solution.py:303
  9.0 15.5 %collective-permute-start = (bf16[400,128]{1,0:T(8,128)(2,1)}, bf16[400,128]{1,0:T(8,128)(2,1)S(1)}, u32[]{:S(2)}, u32[]{:S(2)}) collective-permute-start(bf16[400,128]{1,0:T(8,128)(2,1)} %get-tuple-element.23.refs_0_), channel_id=1, source_target_pairs={{0,8},{8,16},{16,24},{24,32},{32,40},{40,48},{48,56},{56,0},{1,9},... | collective-permute-start | bytes 307208 | tf_op jit(solution)/shard_map/ppermute | solution.py:308
  14.2 13.3 %collective-permute-start.1 = (bf16[400,128]{1,0:T(8,128)(2,1)}, bf16[400,128]{1,0:T(8,128)(2,1)S(1)}, u32[]{:S(2)}, u32[]{:S(2)}) collective-permute-start(bf16[400,128]{1,0:T(8,128)(2,1)} %get-tuple-element.23.refs_0_), channel_id=1, source_target_pairs={{0,56},{8,0},{16,8},{24,16},{32,24},{40,32},{48,40},{56,48},{1,57}... | collective-permute-start | bytes 307208 | tf_op jit(solution)/shard_map/ppermute | solution.py:310
  24.5 9.4 %collective-permute-start.2 = (bf16[400,128]{1,0:T(8,128)(2,1)S(1)}, bf16[400,128]{1,0:T(8,128)(2,1)S(1)}, u32[]{:S(2)}, u32[]{:S(2)}) collective-permute-start(bf16[400,128]{1,0:T(8,128)(2,1)S(1)} %collective-permute-done.refs_1_), channel_id=1, source_target_pairs={{0,8},{8,16},{16,24},{24,32},{32,40},{40,48},{48,56},{56,0},{1,9},... | collective-permute-start | bytes 307208 | tf_op jit(solution)/shard_map/ppermute | solution.py:308
  27.4 10.9 %collective-permute-start.3 = (bf16[400,128]{1,0:T(8,128)(2,1)S(1)}, bf16[400,128]{1,0:T(8,128)(2,1)S(1)}, u32[]{:S(2)}, u32[]{:S(2)}) collective-permute-start(bf16[400,128]{1,0:T(8,128)(2,1)S(1)} %collective-permute-done.1.refs_2_), channel_id=1, source_target_pairs={{0,56},{8,0},{16,8},{24,16},{32,24},{40,32},{48,40},{56,48},{1,57}... | collective-permute-start | bytes 307208 | tf_op jit(solution)/shard_map/ppermute | solution.py:310
  34.0 14.6 %collective-permute-start.4 = (bf16[400,128]{1,0:T(8,128)(2,1)S(1)}, bf16[400,128]{1,0:T(8,128)(2,1)S(1)}, u32[]{:S(2)}, u32[]{:S(2)}) collective-permute-start(bf16[400,128]{1,0:T(8,128)(2,1)S(1)} %collective-permute-done.2.refs_3_), channel_id=1, source_target_pairs={{0,8},{8,16},{16,24},{24,32},{32,40},{40,48},{48,56},{56,0},{1,9},... | collective-permute-start | bytes 307208 | tf_op jit(solution)/shard_map/ppermute | solution.py:308
  38.3 15.7 %collective-permute-start.5 = (bf16[400,128]{1,0:T(8,128)(2,1)S(1)}, bf16[400,128]{1,0:T(8,128)(2,1)S(1)}, u32[]{:S(2)}, u32[]{:S(2)}) collective-permute-start(bf16[400,128]{1,0:T(8,128)(2,1)S(1)} %collective-permute-done.3.refs_4_), channel_id=1, source_target_pairs={{0,56},{8,0},{16,8},{24,16},{32,24},{40,32},{48,40},{56,48},{1,57}... | collective-permute-start | bytes 307208 | tf_op jit(solution)/shard_map/ppermute | solution.py:310
  48.6 10.0 %collective-permute-start.6 = (bf16[400,128]{1,0:T(8,128)(2,1)S(1)}, bf16[400,128]{1,0:T(8,128)(2,1)S(1)}, u32[]{:S(2)}, u32[]{:S(2)}) collective-permute-start(bf16[400,128]{1,0:T(8,128)(2,1)S(1)} %collective-permute-done.4.refs_5_), channel_id=1, source_target_pairs={{0,8},{8,16},{16,24},{24,32},{32,40},{40,48},{48,56},{56,0},{1,9},... | collective-permute-start | bytes 307208 | tf_op jit(solution)/shard_map/ppermute | solution.py:308
  61.7 23.1 %all-to-all-start = ((bf16[8,160,384]{2,1,0:T(8,128)(2,1)}), bf16[8,160,384]{2,1,0:T(8,128)(2,1)S(1)}, u32[]{:S(2)}, u32[]{:S(2)}) async-start(bf16[8,160,384]{2,1,0:T(8,128)(2,1)} %bitcast.3), calls=%async_computation | async-start | bytes 1966080 | tf_op jit(solution)/shard_map/all_to_all | solution.py:334
  78.5 1.3 copy-start.7
  85.8 26.9 %copy-start.4 = (bf16[8,160,384]{2,1,0:T(8,128)(2,1)S(1)}, bf16[8,160,384]{2,1,0:T(8,128)(2,1)}, u32[]{:S(2)}) copy-start(bf16[8,160,384]{2,1,0:T(8,128)(2,1)} %copy-done.3) | copy-start | bytes 2949124
  85.8 26.9 %copy-start.9 = (bf16[1,512,512]{2,1,0:T(8,128)(2,1)S(1)}, bf16[1,512,512]{2,1,0:T(8,128)(2,1)}, u32[]{:S(2)}) copy-start(bf16[1,512,512]{2,1,0:T(8,128)(2,1)} %param.11) | copy-start | bytes 1572868
  85.8 26.9 %copy-start.11 = (bf16[1,512,512]{2,1,0:T(8,128)(2,1)S(1)}, bf16[1,512,512]{2,1,0:T(8,128)(2,1)}, u32[]{:S(2)}) copy-start(bf16[1,512,512]{2,1,0:T(8,128)(2,1)} %param.12) | copy-start | bytes 1572868
  85.8 26.9 %copy-start.13 = (bf16[1,512,512]{2,1,0:T(8,128)(2,1)S(1)}, bf16[1,512,512]{2,1,0:T(8,128)(2,1)}, u32[]{:S(2)}) copy-start(bf16[1,512,512]{2,1,0:T(8,128)(2,1)} %param.13) | copy-start | bytes 1572868
  118.0 20.4 %all-to-all-start.2 = ((bf16[8,160,512]{2,1,0:T(8,128)(2,1)}), bf16[8,160,512]{2,1,0:T(8,128)(2,1)}, u32[]{:S(2)}, u32[]{:S(2)}) async-start(bf16[8,160,512]{2,1,0:T(8,128)(2,1)} %bitcast.10), calls=%async_computation.2 | async-start | bytes 2621440 | tf_op jit(solution)/shard_map/all_to_all | solution.py:340
  122.3 1.2 copy-start.5
  123.5 1.0 copy-start.10
  125.5 1.0 copy-start.14
  136.2 1.1 copy-start
  138.4 21.4 %all-to-all-start.3 = ((bf16[8,160,512]{2,1,0:T(8,128)(2,1)}), bf16[8,160,512]{2,1,0:T(8,128)(2,1)S(1)}, u32[]{:S(2)}, u32[]{:S(2)}) async-start(bf16[8,160,512]{2,1,0:T(8,128)(2,1)} %bitcast.29), calls=%async_computation.3 | async-start | bytes 2621440 | tf_op jit(solution)/shard_map/all_to_all | solution.py:350
  142.9 76.9 %reduce-scatter.2.cloned.1.call-start = ((), (), s32[]{:S(2)}) async-start(), calls=%async_computation.8 | async-start | bytes 2396160 | tf_op jit(solution)/shard_map/reduce_scatter | solution.py:373
  142.9 1.3 copy-start.8
  152.1 1.0 copy-start.1
  159.8 1.3 copy-start.2
  (3 other events, 2.9 us)
Sparse Core Ops, SparseCore 0:
  10.7 67.7 all-gather.1
  163.0 56.7 reduce-scatter.1

commit v3 on v2

--- a/solution.py
+++ b/solution.py
@@ -24,12 +24,13 @@
 SECOND = CUTS - FIRST
 LEAD = FIRST * LANES
 TAIL = SECOND * LANES
-SENT_RING = LEAD + 2 * TOP
+SENT_LEAD = LEAD + 2 * TOP
 SENT_REST = TAIL + WIDTH + 4 * TOP
+EARLY = 256
+MIXED = TAIL + EARLY
 AT_COT = TAIL
 AT_GATES = TAIL + WIDTH
 BACK = 2 * WIDTH + 2 * TOP
-STEPS = [0] + [s for h in range(1, HI // 2) for s in (-h, h)] + [-(HI // 2)]
 ALL = LO * SLOTS
 ROWS = HI * CAP * LO
 MIB = 1024 * 1024
@@ -63,10 +64,10 @@
     )(*args)
 
 
-def pack_kernel(tok, ids, gates, cot, ring_out, rest_out):
+def pack_kernel(tok, ids, gates, cot, lead_out, rest_out):
     for f in range(CUTS):
         cut = slice(f * LANES, (f + 1) * LANES)
-        to, at = (ring_out, f) if f < FIRST else (rest_out, f - FIRST)
+        to, at = (lead_out, f) if f < FIRST else (rest_out, f - FIRST)
         to[at * TOK : (at + 1) * TOK, :] = tok[:, cut]
         rest_out[AT_COT + f * TOK : AT_COT + (f + 1) * TOK, :] = cot[:, cut]
     gate = gates[...]
@@ -74,7 +75,7 @@
     middle = (gate - high).astype(BF).astype(F32)
     low = gate - high - middle
     named = ids[...].astype(F32)
-    ring_out[LEAD : LEAD + 16, :] = jnp.concatenate([named, named], axis=0).astype(BF)
+    lead_out[LEAD : LEAD + 16, :] = jnp.concatenate([named, named], axis=0).astype(BF)
     rest_out[AT_GATES : AT_GATES + 16, :] = jnp.concatenate([high, middle], axis=0).astype(BF)
     rest_out[AT_GATES + 16 : AT_GATES + 32, :] = jnp.concatenate([low, low], axis=0).astype(BF)
 
@@ -102,18 +103,17 @@
         out[to : to + SLOTS, lanes] = rows[e * SLOTS : (e + 1) * SLOTS, :].astype(BF)
 
 
-def first_kernel(first, *refs):
-    blocks, (x_out, rank_out, ids_out, tok_s, pick_s) = refs[:HI], refs[HI:]
+def first_kernel(first, got, x_out, rank_out, ids_out, tok_s, pick_s):
     base = (first[0] * LO).astype(F32)
     upto = upper(GTOK)
     for g in range(GROUPS):
         part = []
         for b in range(PACK):
-            got = blocks[g * PACK + b]
+            at = (g * PACK + b) * SENT_LEAD
             for f in range(FIRST):
                 cut = slice(f * LANES, (f + 1) * LANES)
-                tok_s[b * TOK : (b + 1) * TOK, cut] = got[f * TOK : (f + 1) * TOK, :]
-            part.append(got[LEAD : LEAD + 16, :].astype(F32)[:TOP])
+                tok_s[b * TOK : (b + 1) * TOK, cut] = got[at + f * TOK : at + (f + 1) * TOK, :]
+            part.append(got[at + LEAD : at + LEAD + 16, :].astype(F32)[:TOP])
         ids = jnp.concatenate(part, axis=1)
         ids_out[g * TOP : (g + 1) * TOP, :] = ids
         named = [
@@ -126,28 +126,24 @@
         put_rows(x_out, g, nn(pick_s[...], tok_s[...]), slice(0, LEAD))
 
 
-def source(first, step):
-    return lax.rem(first[0] + step + HI, HI)
-
-
-def rest_group(first, got, group, begin, count, kept):
+def rest_group(got, group, begin, count, kept):
     for b in range(PACK):
-        at = source(first, STEPS[group * PACK + b]) * SENT_REST + begin
+        at = (group * PACK + b) * SENT_REST + begin
         for f in range(count):
-            here = pl.ds(pl.multiple_of(at + f * TOK, 16), TOK)
-            kept[b * TOK : (b + 1) * TOK, f * LANES : (f + 1) * LANES] = got[here, :]
-
-
-def rest_kernel(first, got, rank, ids, out, gate_out, tok_s, cot_s, pick_s):
+            cut = slice(f * LANES, (f + 1) * LANES)
+            kept[b * TOK : (b + 1) * TOK, cut] = got[at + f * TOK : at + (f + 1) * TOK, :]
+
+
+def rest_kernel(first, got, rank, ids, out, late_out, gate_out, tok_s, cot_s, pick_s):
     base = (first[0] * LO).astype(F32)
     for g in range(GROUPS):
-        rest_group(first, got, g, 0, SECOND, tok_s)
-        rest_group(first, got, g, AT_COT, CUTS, cot_s)
+        rest_group(got, g, 0, SECOND, tok_s)
+        rest_group(got, g, AT_COT, CUTS, cot_s)
         part = []
         for b in range(PACK):
-            at = source(first, STEPS[g * PACK + b]) * SENT_REST + AT_GATES
-            one = got[pl.ds(pl.multiple_of(at, 16), 16), :].astype(F32)
-            two = got[pl.ds(pl.multiple_of(at + 16, 16), 16), :].astype(F32)
+            at = (g * PACK + b) * SENT_REST + AT_GATES
+            one = got[at : at + 16, :].astype(F32)
+            two = got[at + 16 : at + 32, :].astype(F32)
             part.append((one[:TOP] + one[TOP:]) + two[:TOP])
         gates = jnp.concatenate(part, axis=1)
         named = ids[g * TOP : (g + 1) * TOP, :]
@@ -163,7 +159,8 @@
             scale.append(jnp.sum(picked * weight[e], axis=1, keepdims=True))
         put_rows(out, g, nn(pick_s[...], tok_s[...]), slice(0, TAIL))
         grads = jnp.concatenate(scale, axis=0) * nn(pick_s[...], cot_s[...])
-        put_rows(out, g, grads, slice(TAIL, TAIL + WIDTH))
+        put_rows(out, g, grads[:, :EARLY], slice(TAIL, MIXED))
+        put_rows(late_out, g, grads[:, EARLY:], slice(0, WIDTH - EARLY))
 
 
 TILE = 160
@@ -195,10 +192,11 @@
     tiles(step)
 
 
-def backward_kernel(x, rest, w_gate, w_up, w_down, out, weight, hidden_s, gate_s, up_s):
+def backward_kernel(x, rest, late, w_gate, w_up, w_down, out, weight, hidden_s, gate_s, up_s):
     def step(rows):
         gate_pre, up_pre, sig, activation, hidden = gated(x, rest, w_gate, w_up, rows)
-        hidden_grad = nt(rest[rows, TAIL:], w_down[...])
+        grads = jnp.concatenate([rest[rows, TAIL:], late[rows, :]], axis=1)
+        hidden_grad = nt(grads, w_down[...])
         slope = sig * (1.0 + gate_pre * (1.0 - sig))
         gate = (hidden_grad * up_pre * slope).astype(BF)
         up = (hidden_grad * activation).astype(BF)
@@ -212,7 +210,8 @@
         at = n * WIDTH
         weight[at : at + LEAD, :] = tn(x[...], side[...]).astype(BF)
         weight[at + LEAD : at + WIDTH, :] = tn(rest[:, :TAIL], side[...]).astype(BF)
-    weight[2 * WIDTH : 3 * WIDTH, :] = tn(hidden_s[...], rest[:, TAIL:]).astype(BF)
+    weight[2 * WIDTH :, :EARLY] = tn(hidden_s[...], rest[:, TAIL:]).astype(BF)
+    weight[2 * WIDTH :, EARLY:] = tn(hidden_s[...], late[...]).astype(BF)
 
 
 def split(value):
@@ -228,7 +227,7 @@
     lane = lax.broadcasted_iota(jnp.int32, (1, ALL), 1)
     place = (lane - SLOTS * lax.div(lane, SLOTS) + 1).astype(F32)
     for g in range(GROUPS):
-        rest_group(first, got, g, AT_COT, CUTS, cot_s)
+        rest_group(got, g, AT_COT, CUTS, cot_s)
         for e in range(LO):
             at = (e * GROUPS + g) * SLOTS
             eo_s[e * SLOTS : (e + 1) * SLOTS, :] = eo[at : at + SLOTS, :]
@@ -249,14 +248,14 @@
         grad_high = grad.astype(BF).astype(F32)
         grad = jnp.concatenate([grad_high, grad - grad_high], axis=0).astype(BF)
         for b in range(PACK):
-            at = source(first, STEPS[g * PACK + b])
+            at = g * PACK + b
             for f in range(CUTS):
                 here = layer[b * TOK : (b + 1) * TOK, f * LANES : (f + 1) * LANES]
                 out[at, f * TOK : (f + 1) * TOK, :] = here.astype(BF)
             out[at, 2 * WIDTH : BACK, :] = grad[:, b * TOK : (b + 1) * TOK]
 
 
-def back_kernel(first, picks, ib, held, out, ib_s, sent_s, sems):
+def back_kernel(picks, ib, held, out, ib_s, sent_s, sems):
     del held
     copies = []
     for g in range(GROUPS):
@@ -271,7 +270,7 @@
                 sent_s[n, f * TOK : (f + 1) * TOK, :] = here.astype(BF)
             copy = pltpu.make_async_copy(
                 sent_s.at[n],
-                out.at[source(first, STEPS[n]), pl.ds(WIDTH, WIDTH), :],
+                out.at[n, pl.ds(WIDTH, WIDTH), :],
                 sems.at[n],
             )
             copy.start()
@@ -294,20 +293,14 @@
     first = lax.axis_index("hi").astype(jnp.int32).reshape(1)
     w_gate, w_up, w_down = w_gate[0], w_up[0], w_down[0]
     square = 2 * ROWS * WIDTH * WIDTH
-    ring_sent, rest_sent = call(
+    lead_sent, rest_sent = call(
         pack_kernel,
-        [shape((SENT_RING, LANES), BF), shape((SENT_REST, LANES), BF)],
+        [shape((SENT_LEAD, LANES), BF), shape((SENT_REST, LANES), BF)],
         [tokens, expert_ids.T, gate_weights.T, cotangent],
         room=56,
     )
     got = lax.all_gather(rest_sent, "hi", axis=0, tiled=True)
-    after = [(i, (i + 1) % HI) for i in range(HI)]
-    before = [(i, (i - 1) % HI) for i in range(HI)]
-    blocks = {0: ring_sent}
-    for h in range(1, HI // 2 + 1):
-        blocks[-h] = lax.ppermute(blocks[1 - h], "hi", after)
-        if h < HI // 2:
-            blocks[h] = lax.ppermute(blocks[h - 1], "hi", before)
+    lead = lax.all_gather(lead_sent, "hi", axis=0, tiled=True)
     picked = pltpu.VMEM((ALL, GTOK), BF)
     rows_first, rank, ids = call(
         first_kernel,
@@ -316,13 +309,17 @@
             shape((GROUPS * LO, GTOK), F32),
             shape((GROUPS * TOP, GTOK), F32),
         ],
-        [first] + [blocks[s] for s in STEPS],
+        [first, lead],
         [pltpu.VMEM((GTOK, LEAD), BF), picked],
         scalars=1,
     )
-    rows_rest, gate = call(
+    rows_rest, rows_late, gate = call(
         rest_kernel,
-        [shape((ROWS, TAIL + WIDTH), BF), shape((GROUPS * LO, GTOK), F32)],
+        [
+            shape((ROWS, MIXED), BF),
+            shape((ROWS, WIDTH - EARLY), BF),
+            shape((GROUPS * LO, GTOK), F32),
+        ],
         [first, got, rank, ids],
         [pltpu.VMEM((GTOK, TAIL), BF), pltpu.VMEM((GTOK, WIDTH), BF), picked],
         scalars=1,
@@ -333,6 +330,7 @@
     )
     x = exchange(rows_first)
     rest = exchange(rows_rest)
+    late = exchange(rows_late)
     narrow = shape((ROWS, WIDTH), BF)
     (expert_out,) = call(
         forward_kernel, [narrow], [x, rest, w_gate, w_up, w_down], flops=3 * square
@@ -342,7 +340,7 @@
     input_back, weight_part = call(
         backward_kernel,
         [narrow, shape((3 * WIDTH, WIDTH), BF)],
-        [x, rest, w_gate, w_up, w_down],
+        [x, rest, late, w_gate, w_up, w_down],
         [whole, whole, whole],
         flops=8 * square,
     )
@@ -359,17 +357,17 @@
     partial = pl.pallas_call(
         back_kernel,
         out_shape=shape((HI, BACK, LANES), BF),
-        in_specs=[SMEM, VMEM, VMEM, pl.BlockSpec(memory_space=pl.ANY)],
+        in_specs=[VMEM, VMEM, pl.BlockSpec(memory_space=pl.ANY)],
         out_specs=pl.BlockSpec(memory_space=pl.ANY),
         scratch_shapes=[
             pltpu.VMEM((ALL, WIDTH), BF),
             pltpu.VMEM((HI, WIDTH, LANES), BF),
             pltpu.SemaphoreType.DMA((HI,)),
         ],
-        input_output_aliases={3: 0},
+        input_output_aliases={2: 0},
         compiler_params=pltpu.CompilerParams(vmem_limit_bytes=24 * MIB),
         cost_estimate=pl.CostEstimate(flops=square, bytes_accessed=4 << 20, transcendentals=0),
-    )(first, picks, ib, partial)
+    )(picks, ib, partial)
     summed = lax.psum_scatter(
         partial.reshape(HI * BACK, LANES), "hi", scatter_dimension=0, tiled=True
     )

time: 230 us -> 229 us (level)
  blocking collectives: 75.3 us -> 111 us
  starting transfers between devices: 50.7 us -> 19.7 us
  waiting for transfers between devices: 42.6 us -> 30.2 us
  local copies, waits for them, and re-layouts: 13.6 us -> 19.9 us
    all_gather x0 -> x1, blocking collectives: none -> 44.3 us  [body(): lead = lax.all_gather(lead_sent, 'hi', axis=0, tiled=True)]
    ppermute x7 -> x0, starting transfers between devices: 33.3 us -> none  [the longest x3 22.3 us: body(): blocks[h] = lax.ppermute(blocks[h - 1], 'hi', before)]
    ppermute x7 -> x0, waiting for transfers between devices: 16.2 us -> none  [the longest x4 9.28 us: body(): blocks[-h] = lax.ppermute(blocks[1 - h], 'hi', after)]
    all_gather x1, waiting for transfers between devices: 8.21 us -> 16.9 us  [body(): got = lax.all_gather(rest_sent, 'hi', axis=0, tiled=True)]
    all_to_all x1, blocking collectives: 26.9 us -> 18.8 us  [body(): rest = exchange(rows_rest)]
    unnamed x30 -> x48, local copies, waits for them, and re-layouts: 12.3 us -> 18.6 us
    all_to_all x1, starting transfers between devices: 8.59 us -> 4.93 us  [body(): x = exchange(rows_first)]
    all_to_all x0 -> x1, starting transfers between devices: none -> 3.54 us  [body(): late = exchange(rows_late)]
  transfers between devices with their start and end apart: 12 -> 6, of which waited for: 12 -> 4; matrix products, arithmetic and copies ran while one was open for 1% -> 1% of each run, Pallas kernels for 9% -> 11%
where the time goes in v3:
time: 229 us; the launch traced here: 226 us
  blocking collectives  111 us (48%)
  Pallas kernels  30.3 us (13%)
  waiting for transfers between devices  30.2 us (13%)
  local copies, waits for them, and re-layouts  19.9 us (9%)
  starting transfers between devices  19.7 us (9%)
  between operations  14.2 us (6%)
    all_gather x1, blocking collectives, body(): lead = lax.all_gather(lead_sent, 'hi', axis=0, tiled=True)  44.3 us
    pallas_call x7, Pallas kernels, call(): pl.pallas_call(kernel, out_shape=shapes, in_specs=[SMEM] * scalars + [VME...  28.5 us
    all_to_all x1, blocking collectives, body(): over_dp(jnp.tile(share, (data, 1))).reshape(3, 1, WIDTH, WIDTH)  24.2 us
    all_to_all x1, blocking collectives, body(): share = over_dp(weight_part).reshape(data, -1, WIDTH).astype(F32)  24 us
    all_to_all x1, blocking collectives, body(): rest = exchange(rows_rest)  18.8 us
    unnamed x48, local copies, waits for them, and re-layouts  18.6 us
    all_gather x1, waiting for transfers between devices, body(): got = lax.all_gather(rest_sent, 'hi', axis=0, tiled=True)  16.9 us
    reduce_scatter x1, waiting for transfers between devices, body(): lax.psum_scatter(partial.reshape(HI * BACK, LANES), 'hi', scatter_dimensi...  9.13 us
  transfers between devices with their start and end apart: 6, of which 4 were waited for; matrix products, arithmetic and copies ran while one was open for 1% of the time, Pallas kernels for 11%

profile of v3, /device:TPU:6, one launch (start us, length us, event | category | flops | bytes accessed | tf_op | source)
XLA Modules:
  0.0 225.9 jit_solution(8482023389232301981)
XLA Ops:
  7.2 1.8 shard_map.118
  9.0 44.3 %all_gather.7.got = bf16[3200,128]{1,0:T(8,128)(2,1)S(1)} all-gather(bf16[400,128]{1,0:T(8,128)(2,1)} %get-tuple-element.24), channel_id=1, replica_groups=mesh['dp'=8,'hi'=8,'lo'=8] {'hi'}, dimensions={0}, use_global_device_ids=true | all-gather | bytes 921600 | tf_op jit(solution)/shard_map/all_gather | solution.py:303
  53.3 2.2 shard_map.119
  55.5 4.9 %all-to-all-start = ((bf16[8,160,384]{2,1,0:T(8,128)(2,1)}), bf16[8,160,384]{2,1,0:T(8,128)(2,1)S(1)}, u32[]{:S(2)}, u32[]{:S(2)}) async-start(bf16[8,160,384]{2,1,0:T(8,128)(2,1)} %bitcast.3), calls=%async_computation | async-start | bytes 1966080 | tf_op jit(solution)/shard_map/all_to_all | solution.py:331
  60.4 16.9 %all-gather.2.cloned.1.call-done.got = bf16[5376,128]{1,0:T(8,128)(2,1)} async-done(((bf16[672,128]{1,0:T(8,128)(2,1)}), bf16[5376,128]{1,0:T(8,128)(2,1)}) %all-gather.2.cloned.1.call-update) | async-done | bytes 1376272 | tf_op jit(solution)/shard_map/all_gather | solution.py:302
  77.4 1.3 copy-done.10
  78.7 1.5 shard_map.120
  81.8 18.8 %all_to_all.74 = bf16[8,160,384]{2,1,0:T(8,128)(2,1)S(1)} all-to-all(bf16[8,160,384]{2,1,0:T(8,128)(2,1)S(1)} %bitcast.34), channel_id=1, replica_groups=mesh['dp'=8,'hi'=8,'lo'=8] {'lo'}, dimensions={0} | all-to-all | bytes 1966080 | tf_op jit(solution)/shard_map/all_to_all | solution.py:332
  100.6 3.5 %all-to-all-start.3 = ((bf16[8,160,256]{2,1,0:T(8,128)(2,1)}), bf16[8,160,256]{2,1,0:T(8,128)(2,1)S(1)}, u32[]{:S(2)}, u32[]{:S(2)}) async-start(bf16[8,160,256]{2,1,0:T(8,128)(2,1)} %bitcast.36), calls=%async_computation.3 | async-start | bytes 1310720 | tf_op jit(solution)/shard_map/all_to_all | solution.py:333
  107.2 5.3 %shard_map.121 = bf16[1280,512]{1,0:T(8,128)(2,1)} custom-call(bf16[1280,384]{1,0:T(8,128)(2,1)S(1)} %bitcast.30, bf16[1280,384]{1,0:T(8,128)(2,1)S(1)} %bitcast.32, bf16[512,512]{1,0:T(8,128)(2,1)S(1)} %bitcast.37, bf16[512,512]{1,0:T(8,128)(2,1)S(1)} %bitcast.39, bf16[512,512]{1,0:T(8,128)(2,1)S(1)} %bitcast.41), custom_call_target="tpu_custom_call" | custom-call | flops 2013265920 | bytes 4849664 | tf_op jit(solution)/shard_map/pallas_call | solution.py:56
  112.8 5.3 %all-to-all-start.2 = ((bf16[8,160,512]{2,1,0:T(8,128)(2,1)}), bf16[8,160,512]{2,1,0:T(8,128)(2,1)S(1)}, u32[]{:S(2)}, u32[]{:S(2)}) async-start(bf16[8,160,512]{2,1,0:T(8,128)(2,1)} %bitcast.10), calls=%async_computation.2 | async-start | bytes 2621440 | tf_op jit(solution)/shard_map/all_to_all | solution.py:338
  119.3 1.2 copy-done.8
  123.7 9.6 %shard_map.122 = (bf16[1280,512]{1,0:T(8,128)(2,1)S(1)}, bf16[1536,512]{1,0:T(8,128)(2,1)S(1)}) custom-call(bf16[1280,384]{1,0:T(8,128)(2,1)S(1)} %bitcast.31, bf16[1280,384]{1,0:T(8,128)(2,1)S(1)} %bitcast.33, bf16[1280,256]{1,0:T(8,128)(2,1)S(1)} %bitcast.35, bf16[512,512]{1,0:T(8,128)(2,1)S(1)} %bitcast.38, bf16[512,512]{1,0:T(8,128)(2,1)S(1)} %bitcast.40, ...), custom_call_target="tpu_custom_call" | custom-call | flops 5368709120 | bytes 7077888 | tf_op jit(solution)/shard_map/pallas_call | solution.py:56
  135.4 5.8 %all-to-all-start.4 = ((bf16[8,160,512]{2,1,0:T(8,128)(2,1)}), bf16[8,160,512]{2,1,0:T(8,128)(2,1)S(1)}, u32[]{:S(2)}, u32[]{:S(2)}) async-start(bf16[8,160,512]{2,1,0:T(8,128)(2,1)} %bitcast.29), calls=%async_computation.4 | async-start | bytes 2621440 | tf_op jit(solution)/shard_map/all_to_all | solution.py:348
  141.3 1.3 copy-done.1
  142.6 1.3 copy-done.11
  144.0 6.4 %shard_map.123 = (bf16[8,1040,128]{2,1,0:T(8,128)(2,1)}, bf16[1024,640]{1,0:T(8,128)(2,1)S(1)}) custom-call(s32[1]{0:T(128)} %bitcast.first, bf16[5376,128]{1,0:T(8,128)(2,1)S(1)} %copy-done.11, f32[16,512]{1,0:T(8,128)S(1)} %copy-done.19, f32[16,512]{1,0:T(8,128)S(1)} %copy-done.21, f32[16,512]{1,0:T(8,128)S(1)} %copy-done.23, bf16[1280,512]{1,0:T(8,128)(2,1)S(1)} %bitcast.28), custom_call_target="tpu_custom_call" | custom-call | flops 2013265920 | bytes 6225924 | tf_op jit(solution)/shard_map/pallas_call | solution.py:56
  151.5 3.8 %all-to-all-done.4 = bf16[8,160,512]{2,1,0:T(8,128)(2,1)S(1)} async-done(((bf16[8,160,512]{2,1,0:T(8,128)(2,1)}), bf16[8,160,512]{2,1,0:T(8,128)(2,1)S(1)}, u32[]{:S(2)}, u32[]{:S(2)}) %all-to-all-start.4) | async-done | bytes 1310752 | tf_op jit(solution)/shard_map/all_to_all | solution.py:348
  155.3 1.3 copy-done.4
  156.6 1.8 shard_map.124
  158.4 24.0 %all_to_all.75 = bf16[8,192,512]{2,1,0:T(8,128)(2,1)S(1)} all-to-all(bf16[8,192,512]{2,1,0:T(8,128)(2,1)S(1)} %bitcast.27), channel_id=1, replica_groups=mesh['dp'=8,'hi'=8,'lo'=8] {'dp'}, dimensions={0} | all-to-all | bytes 3145728 | tf_op jit(solution)/shard_map/all_to_all | solution.py:378
  182.8 24.2 %all_to_all.76 = bf16[8,192,512]{2,1,0:T(8,128)(2,1)S(1)} all-to-all(bf16[8,192,512]{2,1,0:T(8,128)(2,1)S(1)} %tile.2), channel_id=1, replica_groups=mesh['dp'=8,'hi'=8,'lo'=8] {'dp'}, dimensions={0} | all-to-all | bytes 3145728 | tf_op jit(solution)/shard_map/all_to_all | solution.py:381
  208.2 9.1 %reduce-scatter.2.cloned.1.call-done.got = bf16[1040,128]{1,0:T(8,128)(2,1)} async-done(((bf16[8320,128]{1,0:T(8,128)(2,1)}), bf16[1040,128]{1,0:T(8,128)(2,1)}) %reduce-scatter.2.cloned.1.call-update) | async-done | bytes 266256 | tf_op jit(solution)/shard_map/reduce_scatter | solution.py:371
  217.4 1.7 shard_map.125
  (54 shorter events, 14.1 us)
Async XLA Ops:
  7.2 70.2 %all-gather.2.cloned.1.call-start = ((), (), s32[]{:S(2)}) async-start(), calls=%async_computation.8 | async-start | bytes 1548288 | tf_op jit(solution)/shard_map/all_gather | solution.py:302
  55.5 24.8 %copy-start.18 = (f32[16,512]{1,0:T(8,128)}, f32[16,512]{1,0:T(8,128)S(1)}, u32[]{:S(2)}) copy-start(f32[16,512]{1,0:T(8,128)S(1)} %get-tuple-element.25.rank) | copy-start | bytes 98308
  55.5 24.8 %copy-start.20 = (f32[16,512]{1,0:T(8,128)}, f32[16,512]{1,0:T(8,128)S(1)}, u32[]{:S(2)}) copy-start(f32[16,512]{1,0:T(8,128)S(1)} %get-tuple-element.26.ids) | copy-start | bytes 98308
  55.5 26.3 %all-to-all-start = ((bf16[8,160,384]{2,1,0:T(8,128)(2,1)}), bf16[8,160,384]{2,1,0:T(8,128)(2,1)S(1)}, u32[]{:S(2)}, u32[]{:S(2)}) async-start(bf16[8,160,384]{2,1,0:T(8,128)(2,1)} %bitcast.3), calls=%async_computation | async-start | bytes 1966080 | tf_op jit(solution)/shard_map/all_to_all | solution.py:331
  77.4 1.3 copy-start.10
  81.8 22.3 %copy-start.5 = (bf16[8,160,384]{2,1,0:T(8,128)(2,1)}, bf16[8,160,384]{2,1,0:T(8,128)(2,1)S(1)}, u32[]{:S(2)}) copy-start(bf16[8,160,384]{2,1,0:T(8,128)(2,1)S(1)} %all-to-all-done) | copy-start | bytes 2949124
  100.6 12.0 %copy-start.7 = (bf16[8,160,384]{2,1,0:T(8,128)(2,1)}, bf16[8,160,384]{2,1,0:T(8,128)(2,1)S(1)}, u32[]{:S(2)}) copy-start(bf16[8,160,384]{2,1,0:T(8,128)(2,1)S(1)} %all_to_all.74) | copy-start | bytes 2949124
  100.6 12.3 %all-to-all-start.3 = ((bf16[8,160,256]{2,1,0:T(8,128)(2,1)}), bf16[8,160,256]{2,1,0:T(8,128)(2,1)S(1)}, u32[]{:S(2)}, u32[]{:S(2)}) async-start(bf16[8,160,256]{2,1,0:T(8,128)(2,1)} %bitcast.36), calls=%async_computation.3 | async-start | bytes 1310720 | tf_op jit(solution)/shard_map/all_to_all | solution.py:333
  104.1 1.0 copy-start.12
  105.2 1.0 copy-start.14
  106.2 1.0 copy-start.16
  112.8 21.5 %all-to-all-start.2 = ((bf16[8,160,512]{2,1,0:T(8,128)(2,1)}), bf16[8,160,512]{2,1,0:T(8,128)(2,1)S(1)}, u32[]{:S(2)}, u32[]{:S(2)}) async-start(bf16[8,160,512]{2,1,0:T(8,128)(2,1)} %bitcast.10), calls=%async_computation.2 | async-start | bytes 2621440 | tf_op jit(solution)/shard_map/all_to_all | solution.py:338
  118.1 1.2 copy-start.6
  119.3 1.2 copy-start.8
  120.5 1.0 copy-start.13
  133.3 1.1 copy-start.2
  135.4 5.9 %copy-start.19 = (f32[16,512]{1,0:T(8,128)S(1)}, f32[16,512]{1,0:T(8,128)}, u32[]{:S(2)}) copy-start(f32[16,512]{1,0:T(8,128)} %copy-done.18) | copy-start | bytes 98308
  135.4 5.9 %copy-start.21 = (f32[16,512]{1,0:T(8,128)S(1)}, f32[16,512]{1,0:T(8,128)}, u32[]{:S(2)}) copy-start(f32[16,512]{1,0:T(8,128)} %copy-done.20) | copy-start | bytes 98308
  135.4 5.9 %copy-start.23 = (f32[16,512]{1,0:T(8,128)S(1)}, f32[16,512]{1,0:T(8,128)}, u32[]{:S(2)}) copy-start(f32[16,512]{1,0:T(8,128)} %copy-done.22) | copy-start | bytes 98308
  135.4 19.8 %all-to-all-start.4 = ((bf16[8,160,512]{2,1,0:T(8,128)(2,1)}), bf16[8,160,512]{2,1,0:T(8,128)(2,1)S(1)}, u32[]{:S(2)}, u32[]{:S(2)}) async-start(bf16[8,160,512]{2,1,0:T(8,128)(2,1)} %bitcast.29), calls=%async_computation.4 | async-start | bytes 2621440 | tf_op jit(solution)/shard_map/all_to_all | solution.py:348
  141.2 76.1 %reduce-scatter.2.cloned.1.call-start = ((), (), s32[]{:S(2)}) async-start(), calls=%async_computation.9 | async-start | bytes 2396160 | tf_op jit(solution)/shard_map/reduce_scatter | solution.py:371
  141.3 1.3 copy-start.1
  142.6 1.3 copy-start.11
  155.3 1.3 copy-start.4
  (6 other events, 5.7 us)
Sparse Core Ops, SparseCore 0:
  10.7 66.6 all-gather.1
  158.5 58.8 reduce-scatter.1

commit v4 on v3

--- a/solution.py
+++ b/solution.py
@@ -24,16 +24,18 @@
 SECOND = CUTS - FIRST
 LEAD = FIRST * LANES
 TAIL = SECOND * LANES
-SENT_LEAD = LEAD + 2 * TOP
-SENT_REST = TAIL + WIDTH + 4 * TOP
+PART = TOK // 2
+AT_IDS = LEAD + PART
+SENT_LEAD = AT_IDS + 4 * TOP
+SENT_REST = TOK - PART + WIDTH
 EARLY = 256
 MIXED = TAIL + EARLY
-AT_COT = TAIL
-AT_GATES = TAIL + WIDTH
+AT_COT = TOK - PART
 BACK = 2 * WIDTH + 2 * TOP
 ALL = LO * SLOTS
 ROWS = HI * CAP * LO
 MIB = 1024 * 1024
+ROOM = 24
 VMEM = pl.BlockSpec(memory_space=pltpu.VMEM)
 SMEM = pl.BlockSpec(memory_space=pltpu.SMEM)
 
@@ -67,17 +69,18 @@
 def pack_kernel(tok, ids, gates, cot, lead_out, rest_out):
     for f in range(CUTS):
         cut = slice(f * LANES, (f + 1) * LANES)
-        to, at = (lead_out, f) if f < FIRST else (rest_out, f - FIRST)
-        to[at * TOK : (at + 1) * TOK, :] = tok[:, cut]
+        if f < FIRST:
+            lead_out[f * TOK : (f + 1) * TOK, :] = tok[:, cut]
         rest_out[AT_COT + f * TOK : AT_COT + (f + 1) * TOK, :] = cot[:, cut]
+    lead_out[LEAD:AT_IDS, :] = tok[:PART, LEAD:]
+    rest_out[:AT_COT, :] = tok[PART:, LEAD:]
     gate = gates[...]
     high = gate.astype(BF).astype(F32)
     middle = (gate - high).astype(BF).astype(F32)
     low = gate - high - middle
     named = ids[...].astype(F32)
-    lead_out[LEAD : LEAD + 16, :] = jnp.concatenate([named, named], axis=0).astype(BF)
-    rest_out[AT_GATES : AT_GATES + 16, :] = jnp.concatenate([high, middle], axis=0).astype(BF)
-    rest_out[AT_GATES + 16 : AT_GATES + 32, :] = jnp.concatenate([low, low], axis=0).astype(BF)
+    lead_out[AT_IDS : AT_IDS + 16, :] = jnp.concatenate([named, high], axis=0).astype(BF)
+    lead_out[AT_IDS + 16 : SENT_LEAD, :] = jnp.concatenate([middle, low], axis=0).astype(BF)
 
 
 def upper(size):
@@ -103,60 +106,57 @@
         out[to : to + SLOTS, lanes] = rows[e * SLOTS : (e + 1) * SLOTS, :].astype(BF)
 
 
-def first_kernel(first, got, x_out, rank_out, ids_out, tok_s, pick_s):
+def first_kernel(first, got, x_out, rank_out, ids_out, gate_out, tok_s, pick_s):
     base = (first[0] * LO).astype(F32)
     upto = upper(GTOK)
     for g in range(GROUPS):
-        part = []
+        named, weights = [], []
         for b in range(PACK):
             at = (g * PACK + b) * SENT_LEAD
             for f in range(FIRST):
                 cut = slice(f * LANES, (f + 1) * LANES)
                 tok_s[b * TOK : (b + 1) * TOK, cut] = got[at + f * TOK : at + (f + 1) * TOK, :]
-            part.append(got[at + LEAD : at + LEAD + 16, :].astype(F32)[:TOP])
-        ids = jnp.concatenate(part, axis=1)
+            one = got[at + AT_IDS : at + AT_IDS + 16, :].astype(F32)
+            two = got[at + AT_IDS + 16 : at + SENT_LEAD, :].astype(F32)
+            named.append(one[:TOP])
+            weights.append((one[TOP:] + two[:TOP]) + two[TOP:])
+        ids = jnp.concatenate(named, axis=1)
+        weights = jnp.concatenate(weights, axis=1)
         ids_out[g * TOP : (g + 1) * TOP, :] = ids
-        named = [
-            jnp.sum(jnp.where(ids == base + e, 1.0, 0.0), axis=0, keepdims=True)
-            for e in range(LO)
-        ]
+        named, weight = [], []
+        for e in range(LO):
+            same = ids == base + e
+            named.append(jnp.sum(jnp.where(same, 1.0, 0.0), axis=0, keepdims=True))
+            weight.append(jnp.sum(jnp.where(same, weights, 0.0), axis=0, keepdims=True))
         named = jnp.concatenate(named, axis=0)
+        gate_out[g * LO : (g + 1) * LO, :] = jnp.concatenate(weight, axis=0)
         rank_out[g * LO : (g + 1) * LO, :] = named * nn(named.astype(BF), upto)
         pick_rows(rank_out, g, pick_s)
         put_rows(x_out, g, nn(pick_s[...], tok_s[...]), slice(0, LEAD))
 
 
-def rest_group(got, group, begin, count, kept):
+def cotangents(got, group, kept):
     for b in range(PACK):
-        at = (group * PACK + b) * SENT_REST + begin
-        for f in range(count):
+        at = (group * PACK + b) * SENT_REST + AT_COT
+        for f in range(CUTS):
             cut = slice(f * LANES, (f + 1) * LANES)
             kept[b * TOK : (b + 1) * TOK, cut] = got[at + f * TOK : at + (f + 1) * TOK, :]
 
 
-def rest_kernel(first, got, rank, ids, out, late_out, gate_out, tok_s, cot_s, pick_s):
-    base = (first[0] * LO).astype(F32)
+def rest_kernel(lead, got, rank, gate, out, late_out, tok_s, cot_s, pick_s):
     for g in range(GROUPS):
-        rest_group(got, g, 0, SECOND, tok_s)
-        rest_group(got, g, AT_COT, CUTS, cot_s)
-        part = []
+        cotangents(got, g, cot_s)
         for b in range(PACK):
-            at = (g * PACK + b) * SENT_REST + AT_GATES
-            one = got[at : at + 16, :].astype(F32)
-            two = got[at + 16 : at + 32, :].astype(F32)
-            part.append((one[:TOP] + one[TOP:]) + two[:TOP])
-        gates = jnp.concatenate(part, axis=1)
-        named = ids[g * TOP : (g + 1) * TOP, :]
-        weight = [
-            jnp.sum(jnp.where(named == base + e, gates, 0.0), axis=0, keepdims=True)
-            for e in range(LO)
-        ]
-        gate_out[g * LO : (g + 1) * LO, :] = jnp.concatenate(weight, axis=0)
+            at = (g * PACK + b) * SENT_LEAD
+            tok_s[b * TOK : b * TOK + PART, :] = lead[at + LEAD : at + AT_IDS, :]
+            at = (g * PACK + b) * SENT_REST
+            tok_s[b * TOK + PART : (b + 1) * TOK, :] = got[at : at + AT_COT, :]
         pick_rows(rank, g, pick_s)
         scale = []
         for e in range(LO):
             picked = pick_s[e * SLOTS : (e + 1) * SLOTS, :].astype(F32)
-            scale.append(jnp.sum(picked * weight[e], axis=1, keepdims=True))
+            weight = gate[g * LO + e : g * LO + e + 1, :]
+            scale.append(jnp.sum(picked * weight, axis=1, keepdims=True))
         put_rows(out, g, nn(pick_s[...], tok_s[...]), slice(0, TAIL))
         grads = jnp.concatenate(scale, axis=0) * nn(pick_s[...], cot_s[...])
         put_rows(out, g, grads[:, :EARLY], slice(TAIL, MIXED))
@@ -227,7 +227,7 @@
     lane = lax.broadcasted_iota(jnp.int32, (1, ALL), 1)
     place = (lane - SLOTS * lax.div(lane, SLOTS) + 1).astype(F32)
     for g in range(GROUPS):
-        rest_group(got, g, AT_COT, CUTS, cot_s)
+        cotangents(got, g, cot_s)
         for e in range(LO):
             at = (e * GROUPS + g) * SLOTS
             eo_s[e * SLOTS : (e + 1) * SLOTS, :] = eo[at : at + SLOTS, :]
@@ -302,28 +302,21 @@
     got = lax.all_gather(rest_sent, "hi", axis=0, tiled=True)
     lead = lax.all_gather(lead_sent, "hi", axis=0, tiled=True)
     picked = pltpu.VMEM((ALL, GTOK), BF)
-    rows_first, rank, ids = call(
+    small = shape((GROUPS * LO, GTOK), F32)
+    rows_first, rank, ids, gate = call(
         first_kernel,
-        [
-            shape((ROWS, LEAD), BF),
-            shape((GROUPS * LO, GTOK), F32),
-            shape((GROUPS * TOP, GTOK), F32),
-        ],
+        [shape((ROWS, LEAD), BF), small, shape((GROUPS * TOP, GTOK), F32), small],
         [first, lead],
         [pltpu.VMEM((GTOK, LEAD), BF), picked],
         scalars=1,
     )
-    rows_rest, rows_late, gate = call(
+    rows_rest, rows_late = call(
         rest_kernel,
-        [
-            shape((ROWS, MIXED), BF),
-            shape((ROWS, WIDTH - EARLY), BF),
-            shape((GROUPS * LO, GTOK), F32),
-        ],
-        [first, got, rank, ids],
+        [shape((ROWS, MIXED), BF), shape((ROWS, WIDTH - EARLY), BF)],
+        [lead, got, rank, gate],
         [pltpu.VMEM((GTOK, TAIL), BF), pltpu.VMEM((GTOK, WIDTH), BF), picked],
-        scalars=1,
         flops=100 * square,
+        room=ROOM,
     )
     exchange = functools.partial(
         lax.all_to_all, axis_name="lo", split_axis=0, concat_axis=0, tiled=True
@@ -343,6 +336,7 @@
         [x, rest, late, w_gate, w_up, w_down],
         [whole, whole, whole],
         flops=8 * square,
+        room=ROOM,
     )
     eo, input_back = lax.optimization_barrier((eo, input_back))
     ib = exchange(input_back)
@@ -352,6 +346,7 @@
         [first, got, rank, ids, gate, eo],
         [pltpu.VMEM((GTOK, WIDTH), BF), pltpu.VMEM((ALL, WIDTH), BF)],
         scalars=1,
+        room=ROOM,
         flops=3 * square,
     )
     partial = pl.pallas_call(

time: 229 us -> 225 us (0.983)
  waiting for transfers between devices: 30.2 us -> 26.5 us
    all_gather x1, waiting for transfers between devices: 16.9 us -> 11.9 us  [body(): got = lax.all_gather(rest_sent, 'hi', axis=0, tiled=True)]
    all_gather x1, blocking collectives: 44.3 us -> 46.7 us  [body(): lead = lax.all_gather(lead_sent, 'hi', axis=0, tiled=True)]
  transfers between devices with their start and end apart: 6 -> 6, of which waited for: 4 -> 5; matrix products, arithmetic and copies ran while one was open for 1% -> 1% of each run, Pallas kernels for 11% -> 11%
where the time goes in v4:
time: 225 us; the launch traced here: 222 us
  blocking collectives  113 us (50%)
  Pallas kernels  30.3 us (13%)
  waiting for transfers between devices  26.5 us (12%)
  local copies, waits for them, and re-layouts  19.8 us (9%)
  starting transfers between devices  18.7 us (8%)
  between operations  14.2 us (6%)
    all_gather x1, blocking collectives, body(): lead = lax.all_gather(lead_sent, 'hi', axis=0, tiled=True)  46.7 us
    pallas_call x7, Pallas kernels, call(): pl.pallas_call(kernel, out_shape=shapes, in_specs=[SMEM] * scalars + [VME...  28.5 us
    all_to_all x1, blocking collectives, body(): over_dp(jnp.tile(share, (data, 1))).reshape(3, 1, WIDTH, WIDTH)  24.2 us
    all_to_all x1, blocking collectives, body(): share = over_dp(weight_part).reshape(data, -1, WIDTH).astype(F32)  24 us
    unnamed x48, local copies, waits for them, and re-layouts  18.5 us
    all_to_all x1, blocking collectives, body(): rest = exchange(rows_rest)  17.6 us
    all_gather x1, waiting for transfers between devices, body(): got = lax.all_gather(rest_sent, 'hi', axis=0, tiled=True)  11.9 us
    reduce_scatter x1, waiting for transfers between devices, body(): lax.psum_scatter(partial.reshape(HI * BACK, LANES), 'hi', scatter_dimensi...  8.43 us
  transfers between devices with their start and end apart: 6, of which 5 were waited for; matrix products, arithmetic and copies ran while one was open for 1% of the time, Pallas kernels for 11%

profile of v4, /device:TPU:6, one launch (start us, length us, event | category | flops | bytes accessed | tf_op | source)
XLA Modules:
  0.0 222.3 jit_solution(6214913169645658754)
XLA Ops:
  7.2 1.7 shard_map.118
  9.0 46.7 %all_gather.7.got.lead = bf16[3840,128]{1,0:T(8,128)(2,1)S(1)} all-gather(bf16[480,128]{1,0:T(8,128)(2,1)} %get-tuple-element.24), channel_id=1, replica_groups=mesh['dp'=8,'hi'=8,'lo'=8] {'hi'}, dimensions={0}, use_global_device_ids=true | all-gather | bytes 1105920 | tf_op jit(solution)/shard_map/all_gather | solution.py:303
  55.7 2.3 %shard_map.119 = (bf16[1280,384]{1,0:T(8,128)(2,1)}, f32[16,512]{1,0:T(8,128)S(1)}, f32[16,512]{1,0:T(8,128)S(1)}, f32[16,512]{1,0:T(8,128)S(1)}) custom-call(s32[1]{0:T(128)} %bitcast.first, bf16[3840,128]{1,0:T(8,128)(2,1)S(1)} %all_gather.7.got.lead), custom_call_target="tpu_custom_call" | custom-call | bytes 2064388 | tf_op jit(solution)/shard_map/pallas_call | solution.py:58
  58.6 4.3 %all-to-all-start = ((bf16[8,160,384]{2,1,0:T(8,128)(2,1)}), bf16[8,160,384]{2,1,0:T(8,128)(2,1)S(1)}, u32[]{:S(2)}, u32[]{:S(2)}) async-start(bf16[8,160,384]{2,1,0:T(8,128)(2,1)} %bitcast.3), calls=%async_computation | async-start | bytes 1966080 | tf_op jit(solution)/shard_map/all_to_all | solution.py:324
  62.9 11.9 %all-gather.2.cloned.1.call-done.got = bf16[4608,128]{1,0:T(8,128)(2,1)} async-done(((bf16[576,128]{1,0:T(8,128)(2,1)}), bf16[4608,128]{1,0:T(8,128)(2,1)}) %all-gather.2.cloned.1.call-update) | async-done | bytes 1179664 | tf_op jit(solution)/shard_map/all_gather | solution.py:302
  74.7 1.3 copy-done.10
  76.0 1.5 shard_map.120
  79.5 17.6 %all_to_all.74 = bf16[8,160,384]{2,1,0:T(8,128)(2,1)S(1)} all-to-all(bf16[8,160,384]{2,1,0:T(8,128)(2,1)S(1)} %bitcast.34), channel_id=1, replica_groups=mesh['dp'=8,'hi'=8,'lo'=8] {'lo'}, dimensions={0} | all-to-all | bytes 1966080 | tf_op jit(solution)/shard_map/all_to_all | solution.py:325
  97.1 3.5 %all-to-all-start.3 = ((bf16[8,160,256]{2,1,0:T(8,128)(2,1)}), bf16[8,160,256]{2,1,0:T(8,128)(2,1)S(1)}, u32[]{:S(2)}, u32[]{:S(2)}) async-start(bf16[8,160,256]{2,1,0:T(8,128)(2,1)} %bitcast.36), calls=%async_computation.3 | async-start | bytes 1310720 | tf_op jit(solution)/shard_map/all_to_all | solution.py:326
  103.8 5.3 %shard_map.121 = bf16[1280,512]{1,0:T(8,128)(2,1)} custom-call(bf16[1280,384]{1,0:T(8,128)(2,1)S(1)} %bitcast.30, bf16[1280,384]{1,0:T(8,128)(2,1)S(1)} %bitcast.32, bf16[512,512]{1,0:T(8,128)(2,1)S(1)} %bitcast.37, bf16[512,512]{1,0:T(8,128)(2,1)S(1)} %bitcast.39, bf16[512,512]{1,0:T(8,128)(2,1)S(1)} %bitcast.41), custom_call_target="tpu_custom_call" | custom-call | flops 2013265920 | bytes 4849664 | tf_op jit(solution)/shard_map/pallas_call | solution.py:58
  109.6 5.1 %all-to-all-start.2 = ((bf16[8,160,512]{2,1,0:T(8,128)(2,1)}), bf16[8,160,512]{2,1,0:T(8,128)(2,1)S(1)}, u32[]{:S(2)}, u32[]{:S(2)}) async-start(bf16[8,160,512]{2,1,0:T(8,128)(2,1)} %bitcast.10), calls=%async_computation.2 | async-start | bytes 2621440 | tf_op jit(solution)/shard_map/all_to_all | solution.py:331
  115.9 1.2 copy-done.8
  120.3 9.6 %shard_map.122 = (bf16[1280,512]{1,0:T(8,128)(2,1)S(1)}, bf16[1536,512]{1,0:T(8,128)(2,1)S(1)}) custom-call(bf16[1280,384]{1,0:T(8,128)(2,1)S(1)} %bitcast.31, bf16[1280,384]{1,0:T(8,128)(2,1)S(1)} %bitcast.33, bf16[1280,256]{1,0:T(8,128)(2,1)S(1)} %bitcast.35, bf16[512,512]{1,0:T(8,128)(2,1)S(1)} %bitcast.38, bf16[512,512]{1,0:T(8,128)(2,1)S(1)} %bitcast.40, ...), custom_call_target="tpu_custom_call" | custom-call | flops 5368709120 | bytes 7077888 | tf_op jit(solution)/shard_map/pallas_call | solution.py:58
  132.0 5.7 %all-to-all-start.4 = ((bf16[8,160,512]{2,1,0:T(8,128)(2,1)}), bf16[8,160,512]{2,1,0:T(8,128)(2,1)S(1)}, u32[]{:S(2)}, u32[]{:S(2)}) async-start(bf16[8,160,512]{2,1,0:T(8,128)(2,1)} %bitcast.29), calls=%async_computation.4 | async-start | bytes 2621440 | tf_op jit(solution)/shard_map/all_to_all | solution.py:342
  137.8 1.3 copy-done.1
  139.1 1.3 copy-done.11
  140.4 6.4 %shard_map.123 = (bf16[8,1040,128]{2,1,0:T(8,128)(2,1)}, bf16[1024,640]{1,0:T(8,128)(2,1)S(1)}) custom-call(s32[1]{0:T(128)} %bitcast.first, bf16[4608,128]{1,0:T(8,128)(2,1)S(1)} %copy-done.11, f32[16,512]{1,0:T(8,128)S(1)} %copy-done.19, f32[16,512]{1,0:T(8,128)S(1)} %copy-done.21, f32[16,512]{1,0:T(8,128)S(1)} %copy-done.23, bf16[1280,512]{1,0:T(8,128)(2,1)S(1)} %bitcast.28), custom_call_target="tpu_custom_call" | custom-call | flops 2013265920 | bytes 6029316 | tf_op jit(solution)/shard_map/pallas_call | solution.py:58
  147.9 4.5 %all-to-all-done.4 = bf16[8,160,512]{2,1,0:T(8,128)(2,1)S(1)} async-done(((bf16[8,160,512]{2,1,0:T(8,128)(2,1)}), bf16[8,160,512]{2,1,0:T(8,128)(2,1)S(1)}, u32[]{:S(2)}, u32[]{:S(2)}) %all-to-all-start.4) | async-done | bytes 1310752 | tf_op jit(solution)/shard_map/all_to_all | solution.py:342
  152.4 1.3 copy-done.4
  153.7 1.8 shard_map.124
  155.5 24.0 %all_to_all.75 = bf16[8,192,512]{2,1,0:T(8,128)(2,1)S(1)} all-to-all(bf16[8,192,512]{2,1,0:T(8,128)(2,1)S(1)} %bitcast.27), channel_id=1, replica_groups=mesh['dp'=8,'hi'=8,'lo'=8] {'dp'}, dimensions={0} | all-to-all | bytes 3145728 | tf_op jit(solution)/shard_map/all_to_all | solution.py:373
  179.9 24.2 %all_to_all.76 = bf16[8,192,512]{2,1,0:T(8,128)(2,1)S(1)} all-to-all(bf16[8,192,512]{2,1,0:T(8,128)(2,1)S(1)} %tile.2), channel_id=1, replica_groups=mesh['dp'=8,'hi'=8,'lo'=8] {'dp'}, dimensions={0} | all-to-all | bytes 3145728 | tf_op jit(solution)/shard_map/all_to_all | solution.py:376
  205.3 8.4 %reduce-scatter.2.cloned.1.call-done.got = bf16[1040,128]{1,0:T(8,128)(2,1)} async-done(((bf16[8320,128]{1,0:T(8,128)(2,1)}), bf16[1040,128]{1,0:T(8,128)(2,1)}) %reduce-scatter.2.cloned.1.call-update) | async-done | bytes 266256 | tf_op jit(solution)/shard_map/reduce_scatter | solution.py:366
  213.8 1.7 shard_map.125
  (54 shorter events, 15.5 us)
Async XLA Ops:
  7.2 67.6 %all-gather.2.cloned.1.call-start = ((), (), s32[]{:S(2)}) async-start(), calls=%async_computation.8 | async-start | bytes 1327104 | tf_op jit(solution)/shard_map/all_gather | solution.py:302
  58.6 18.9 %copy-start.18 = (f32[16,512]{1,0:T(8,128)}, f32[16,512]{1,0:T(8,128)S(1)}, u32[]{:S(2)}) copy-start(f32[16,512]{1,0:T(8,128)S(1)} %get-tuple-element.25.rank) | copy-start | bytes 98308
  58.6 18.9 %copy-start.22 = (f32[16,512]{1,0:T(8,128)}, f32[16,512]{1,0:T(8,128)S(1)}, u32[]{:S(2)}) copy-start(f32[16,512]{1,0:T(8,128)S(1)} %get-tuple-element.27.gate) | copy-start | bytes 98308
  58.6 20.9 %all-to-all-start = ((bf16[8,160,384]{2,1,0:T(8,128)(2,1)}), bf16[8,160,384]{2,1,0:T(8,128)(2,1)S(1)}, u32[]{:S(2)}, u32[]{:S(2)}) async-start(bf16[8,160,384]{2,1,0:T(8,128)(2,1)} %bitcast.3), calls=%async_computation | async-start | bytes 1966080 | tf_op jit(solution)/shard_map/all_to_all | solution.py:324
  74.7 1.3 copy-start.10
  79.5 21.1 %copy-start.5 = (bf16[8,160,384]{2,1,0:T(8,128)(2,1)}, bf16[8,160,384]{2,1,0:T(8,128)(2,1)S(1)}, u32[]{:S(2)}) copy-start(bf16[8,160,384]{2,1,0:T(8,128)(2,1)S(1)} %all-to-all-done) | copy-start | bytes 2949124
  97.1 12.0 %copy-start.7 = (bf16[8,160,384]{2,1,0:T(8,128)(2,1)}, bf16[8,160,384]{2,1,0:T(8,128)(2,1)S(1)}, u32[]{:S(2)}) copy-start(bf16[8,160,384]{2,1,0:T(8,128)(2,1)S(1)} %all_to_all.74) | copy-start | bytes 2949124
  97.1 12.5 %all-to-all-start.3 = ((bf16[8,160,256]{2,1,0:T(8,128)(2,1)}), bf16[8,160,256]{2,1,0:T(8,128)(2,1)S(1)}, u32[]{:S(2)}, u32[]{:S(2)}) async-start(bf16[8,160,256]{2,1,0:T(8,128)(2,1)} %bitcast.36), calls=%async_computation.3 | async-start | bytes 1310720 | tf_op jit(solution)/shard_map/all_to_all | solution.py:326
  100.6 1.0 copy-start.12
  101.7 1.0 copy-start.14
  102.7 1.0 copy-start.16
  109.6 21.3 %all-to-all-start.2 = ((bf16[8,160,512]{2,1,0:T(8,128)(2,1)}), bf16[8,160,512]{2,1,0:T(8,128)(2,1)S(1)}, u32[]{:S(2)}, u32[]{:S(2)}) async-start(bf16[8,160,512]{2,1,0:T(8,128)(2,1)} %bitcast.10), calls=%async_computation.2 | async-start | bytes 2621440 | tf_op jit(solution)/shard_map/all_to_all | solution.py:331
  114.7 1.2 copy-start.6
  115.9 1.2 copy-start.8
  129.9 1.1 copy-start.2
  131.0 6.8 %copy-start.19 = (f32[16,512]{1,0:T(8,128)S(1)}, f32[16,512]{1,0:T(8,128)}, u32[]{:S(2)}) copy-start(f32[16,512]{1,0:T(8,128)} %copy-done.18) | copy-start | bytes 98308
  131.0 6.8 %copy-start.21 = (f32[16,512]{1,0:T(8,128)S(1)}, f32[16,512]{1,0:T(8,128)}, u32[]{:S(2)}) copy-start(f32[16,512]{1,0:T(8,128)} %copy-done.20) | copy-start | bytes 98308
  131.0 6.8 %copy-start.23 = (f32[16,512]{1,0:T(8,128)S(1)}, f32[16,512]{1,0:T(8,128)}, u32[]{:S(2)}) copy-start(f32[16,512]{1,0:T(8,128)} %copy-done.22) | copy-start | bytes 98308
  131.0 1.1 copy-start
  132.0 20.3 %all-to-all-start.4 = ((bf16[8,160,512]{2,1,0:T(8,128)(2,1)}), bf16[8,160,512]{2,1,0:T(8,128)(2,1)S(1)}, u32[]{:S(2)}, u32[]{:S(2)}) async-start(bf16[8,160,512]{2,1,0:T(8,128)(2,1)} %bitcast.29), calls=%async_computation.4 | async-start | bytes 2621440 | tf_op jit(solution)/shard_map/all_to_all | solution.py:342
  137.7 76.0 %reduce-scatter.2.cloned.1.call-start = ((), (), s32[]{:S(2)}) async-start(), calls=%async_computation.9 | async-start | bytes 2396160 | tf_op jit(solution)/shard_map/reduce_scatter | solution.py:366
  137.8 1.3 copy-start.1
  139.1 1.3 copy-start.11
  152.4 1.3 copy-start.4
  (6 other events, 5.6 us)
Sparse Core Ops, SparseCore 0:
  10.7 64.0 all-gather.1
  155.6 58.1 reduce-scatter.1

commit v5 on v4

--- a/solution.py
+++ b/solution.py
@@ -336,7 +336,7 @@
         [x, rest, late, w_gate, w_up, w_down],
         [whole, whole, whole],
         flops=8 * square,
-        room=ROOM,
+        room=56,
     )
     eo, input_back = lax.optimization_barrier((eo, input_back))
     ib = exchange(input_back)

time: 225 us -> 222 us (0.987)
  local copies, waits for them, and re-layouts: 19.8 us -> 10.5 us
  waiting for transfers between devices: 26.5 us -> 34.3 us
  Pallas kernels: 30.3 us -> 33.6 us
  starting transfers between devices: 18.7 us -> 15.6 us
    unnamed x48 -> x28, local copies, waits for them, and re-layouts: 18.5 us -> 9.2 us
    all_to_all x1, waiting for transfers between devices: 4.48 us -> 8.82 us  [body(): ib = exchange(input_back)]
    pallas_call x7, Pallas kernels: 28.5 us -> 31.9 us  [call(): pl.pallas_call(kernel, out_shape=shapes, in_specs=[SMEM] * scalars + [VME...]
    all_to_all x1, waiting for transfers between devices: 0.01 us -> 2.44 us  [body(): eo = exchange(expert_out)]
  transfers between devices with their start and end apart: 6 -> 6, of which waited for: 5 -> 6; matrix products, arithmetic and copies ran while one was open for 1% -> 1% of each run, Pallas kernels for 11% -> 13%
where the time goes in v5:
time: 222 us; the launch traced here: 221 us
  blocking collectives  113 us (51%)
  waiting for transfers between devices  34.3 us (15%)
  Pallas kernels  33.6 us (15%)
  starting transfers between devices  15.6 us (7%)
  between operations  14.2 us (6%)
  local copies, waits for them, and re-layouts  10.5 us (5%)
    all_gather x1, blocking collectives, body(): lead = lax.all_gather(lead_sent, 'hi', axis=0, tiled=True)  46.7 us
    pallas_call x7, Pallas kernels, call(): pl.pallas_call(kernel, out_shape=shapes, in_specs=[SMEM] * scalars + [VME...  31.9 us
    all_to_all x1, blocking collectives, body(): over_dp(jnp.tile(share, (data, 1))).reshape(3, 1, WIDTH, WIDTH)  24.2 us
    all_to_all x1, blocking collectives, body(): share = over_dp(weight_part).reshape(data, -1, WIDTH).astype(F32)  24 us
    all_to_all x1, blocking collectives, body(): rest = exchange(rows_rest)  17.7 us
    all_gather x1, waiting for transfers between devices, body(): got = lax.all_gather(rest_sent, 'hi', axis=0, tiled=True)  12.7 us
    unnamed x28, local copies, waits for them, and re-layouts  9.2 us
    all_to_all x1, waiting for transfers between devices, body(): ib = exchange(input_back)  8.82 us
  transfers between devices with their start and end apart: 6, of which 6 were waited for; matrix products, arithmetic and copies ran while one was open for 1% of the time, Pallas kernels for 13%

profile of v5, /device:TPU:6, one launch (start us, length us, event | category | flops | bytes accessed | tf_op | source)
XLA Modules:
  0.0 221.2 jit_solution(14672160268863208039)
XLA Ops:
  7.2 1.7 shard_map.118
  9.0 46.7 %all_gather.7.got.lead = bf16[3840,128]{1,0:T(8,128)(2,1)S(1)} all-gather(bf16[480,128]{1,0:T(8,128)(2,1)} %get-tuple-element.24), channel_id=1, replica_groups=mesh['dp'=8,'hi'=8,'lo'=8] {'hi'}, dimensions={0}, use_global_device_ids=true | all-gather | bytes 1105920 | tf_op jit(solution)/shard_map/all_gather | solution.py:303
  55.7 2.2 %shard_map.119 = (bf16[1280,384]{1,0:T(8,128)(2,1)}, f32[16,512]{1,0:T(8,128)S(1)}, f32[16,512]{1,0:T(8,128)S(1)}, f32[16,512]{1,0:T(8,128)S(1)}) custom-call(s32[1]{0:T(128)} %bitcast.first, bf16[3840,128]{1,0:T(8,128)(2,1)S(1)} %all_gather.7.got.lead), custom_call_target="tpu_custom_call" | custom-call | bytes 2064388 | tf_op jit(solution)/shard_map/pallas_call | solution.py:58
  58.0 4.3 %all-to-all-start = ((bf16[8,160,384]{2,1,0:T(8,128)(2,1)}), bf16[8,160,384]{2,1,0:T(8,128)(2,1)S(1)}, u32[]{:S(2)}, u32[]{:S(2)}) async-start(bf16[8,160,384]{2,1,0:T(8,128)(2,1)} %bitcast.3), calls=%async_computation | async-start | bytes 1966080 | tf_op jit(solution)/shard_map/all_to_all | solution.py:324
  62.2 12.7 %all-gather.2.cloned.1.call-done.got = bf16[4608,128]{1,0:T(8,128)(2,1)} async-done(((bf16[576,128]{1,0:T(8,128)(2,1)}), bf16[4608,128]{1,0:T(8,128)(2,1)}) %all-gather.2.cloned.1.call-update) | async-done | bytes 1179664 | tf_op jit(solution)/shard_map/all_gather | solution.py:302
  75.0 1.3 copy-done.5
  76.2 1.5 shard_map.120
  79.5 17.7 %all_to_all.74 = bf16[8,160,384]{2,1,0:T(8,128)(2,1)S(1)} all-to-all(bf16[8,160,384]{2,1,0:T(8,128)(2,1)S(1)} %bitcast.32), channel_id=1, replica_groups=mesh['dp'=8,'hi'=8,'lo'=8] {'lo'}, dimensions={0} | all-to-all | bytes 1966080 | tf_op jit(solution)/shard_map/all_to_all | solution.py:325
  97.2 3.5 %all-to-all-start.3 = ((bf16[8,160,256]{2,1,0:T(8,128)(2,1)}), bf16[8,160,256]{2,1,0:T(8,128)(2,1)S(1)}, u32[]{:S(2)}, u32[]{:S(2)}) async-start(bf16[8,160,256]{2,1,0:T(8,128)(2,1)} %bitcast.33), calls=%async_computation.3 | async-start | bytes 1310720 | tf_op jit(solution)/shard_map/all_to_all | solution.py:326
  102.9 5.3 %shard_map.121 = bf16[1280,512]{1,0:T(8,128)(2,1)} custom-call(bf16[1280,384]{1,0:T(8,128)(2,1)S(1)} %bitcast.28, bf16[1280,384]{1,0:T(8,128)(2,1)S(1)} %bitcast.30, bf16[512,512]{1,0:T(8,128)(2,1)S(1)} %bitcast.35, bf16[512,512]{1,0:T(8,128)(2,1)S(1)} %bitcast.37, bf16[512,512]{1,0:T(8,128)(2,1)S(1)} %bitcast.39), custom_call_target="tpu_custom_call" | custom-call | flops 2013265920 | bytes 4849664 | tf_op jit(solution)/shard_map/pallas_call | solution.py:58
  108.2 1.5 all-to-all-done.3
  109.7 4.1 %all-to-all-start.2 = ((bf16[8,160,512]{2,1,0:T(8,128)(2,1)}), bf16[8,160,512]{2,1,0:T(8,128)(2,1)S(1)}, u32[]{:S(2)}, u32[]{:S(2)}) async-start(bf16[8,160,512]{2,1,0:T(8,128)(2,1)} %bitcast.10), calls=%async_computation.2 | async-start | bytes 2621440 | tf_op jit(solution)/shard_map/all_to_all | solution.py:331
  113.8 13.0 %shard_map.122 = (bf16[1280,512]{1,0:T(8,128)(2,1)}, bf16[1536,512]{1,0:T(8,128)(2,1)}) custom-call(bf16[1280,384]{1,0:T(8,128)(2,1)} %bitcast.29, bf16[1280,384]{1,0:T(8,128)(2,1)} %bitcast.31, bf16[1280,256]{1,0:T(8,128)(2,1)} %bitcast.43, bf16[512,512]{1,0:T(8,128)(2,1)} %bitcast.34, bf16[512,512]{1,0:T(8,128)(2,1)} %bitcast.36, bf16[512,512]{1,0:T(8,128)(2,1)} %bitcast.38), custom_call_target="tpu_custom_call" | custom-call | flops 5368709120 | bytes 7077888 | tf_op jit(solution)/shard_map/pallas_call | solution.py:58
  126.8 2.4 %all-to-all-done.2 = bf16[8,160,512]{2,1,0:T(8,128)(2,1)S(1)} async-done(((bf16[8,160,512]{2,1,0:T(8,128)(2,1)}), bf16[8,160,512]{2,1,0:T(8,128)(2,1)S(1)}, u32[]{:S(2)}, u32[]{:S(2)}) %all-to-all-start.2) | async-done | bytes 1310752 | tf_op jit(solution)/shard_map/all_to_all | solution.py:331
  129.3 3.6 %all-to-all-start.4 = ((bf16[8,160,512]{2,1,0:T(8,128)(2,1)}), bf16[8,160,512]{2,1,0:T(8,128)(2,1)S(1)}, u32[]{:S(2)}, u32[]{:S(2)}) async-start(bf16[8,160,512]{2,1,0:T(8,128)(2,1)} %bitcast.42), calls=%async_computation.4 | async-start | bytes 2621440 | tf_op jit(solution)/shard_map/all_to_all | solution.py:342
  134.2 6.4 %shard_map.123 = (bf16[8,1040,128]{2,1,0:T(8,128)(2,1)}, bf16[1024,640]{1,0:T(8,128)(2,1)S(1)}) custom-call(s32[1]{0:T(128)} %bitcast.first, bf16[4608,128]{1,0:T(8,128)(2,1)S(1)} %copy-done.6, f32[16,512]{1,0:T(8,128)S(1)} %get-tuple-element.25.rank, f32[16,512]{1,0:T(8,128)S(1)} %get-tuple-element.26.ids, f32[16,512]{1,0:T(8,128)S(1)} %copy-done.11, ...), custom_call_target="tpu_custom_call" | custom-call | flops 2013265920 | bytes 6029316 | tf_op jit(solution)/shard_map/pallas_call | solution.py:58
  141.7 8.8 %all-to-all-done.4 = bf16[8,160,512]{2,1,0:T(8,128)(2,1)S(1)} async-done(((bf16[8,160,512]{2,1,0:T(8,128)(2,1)}), bf16[8,160,512]{2,1,0:T(8,128)(2,1)S(1)}, u32[]{:S(2)}, u32[]{:S(2)}) %all-to-all-start.4) | async-done | bytes 1310752 | tf_op jit(solution)/shard_map/all_to_all | solution.py:342
  150.5 1.3 copy-done.1
  151.8 1.7 shard_map.124
  153.6 1.4 copy-done.12
  155.0 24.0 %all_to_all.75 = bf16[8,192,512]{2,1,0:T(8,128)(2,1)S(1)} all-to-all(bf16[8,192,512]{2,1,0:T(8,128)(2,1)S(1)} %bitcast.41), channel_id=1, replica_groups=mesh['dp'=8,'hi'=8,'lo'=8] {'dp'}, dimensions={0} | all-to-all | bytes 3145728 | tf_op jit(solution)/shard_map/all_to_all | solution.py:373
  179.4 24.2 %all_to_all.76 = bf16[8,192,512]{2,1,0:T(8,128)(2,1)S(1)} all-to-all(bf16[8,192,512]{2,1,0:T(8,128)(2,1)S(1)} %tile.2), channel_id=1, replica_groups=mesh['dp'=8,'hi'=8,'lo'=8] {'dp'}, dimensions={0} | all-to-all | bytes 3145728 | tf_op jit(solution)/shard_map/all_to_all | solution.py:376
  204.8 7.8 %reduce-scatter.2.cloned.1.call-done.got = bf16[1040,128]{1,0:T(8,128)(2,1)} async-done(((bf16[8320,128]{1,0:T(8,128)(2,1)}), bf16[1040,128]{1,0:T(8,128)(2,1)}) %reduce-scatter.2.cloned.1.call-update) | async-done | bytes 266256 | tf_op jit(solution)/shard_map/reduce_scatter | solution.py:366
  212.7 1.7 shard_map.125
  (34 shorter events, 7.9 us)
Async XLA Ops:
  7.2 67.8 %all-gather.2.cloned.1.call-start = ((), (), s32[]{:S(2)}) async-start(), calls=%async_computation.8 | async-start | bytes 1327104 | tf_op jit(solution)/shard_map/all_gather | solution.py:302
  58.0 19.7 %copy-start.10 = (f32[16,512]{1,0:T(8,128)}, f32[16,512]{1,0:T(8,128)S(1)}, u32[]{:S(2)}) copy-start(f32[16,512]{1,0:T(8,128)S(1)} %get-tuple-element.27.gate) | copy-start | bytes 98308
  58.0 21.5 %all-to-all-start = ((bf16[8,160,384]{2,1,0:T(8,128)(2,1)}), bf16[8,160,384]{2,1,0:T(8,128)(2,1)S(1)}, u32[]{:S(2)}, u32[]{:S(2)}) async-start(bf16[8,160,384]{2,1,0:T(8,128)(2,1)} %bitcast.3), calls=%async_computation | async-start | bytes 1966080 | tf_op jit(solution)/shard_map/all_to_all | solution.py:324
  75.0 1.3 copy-start.5
  77.7 0.8 copy-start.4
  79.5 21.3 %copy-start.2 = (bf16[8,160,384]{2,1,0:T(8,128)(2,1)}, bf16[8,160,384]{2,1,0:T(8,128)(2,1)S(1)}, u32[]{:S(2)}) copy-start(bf16[8,160,384]{2,1,0:T(8,128)(2,1)S(1)} %all-to-all-done) | copy-start | bytes 2949124
  79.5 21.3 %copy-start.7 = (bf16[1,512,512]{2,1,0:T(8,128)(2,1)S(1)}, bf16[1,512,512]{2,1,0:T(8,128)(2,1)}, u32[]{:S(2)}) copy-start(bf16[1,512,512]{2,1,0:T(8,128)(2,1)} %param.11) | copy-start | bytes 1572868
  97.2 11.0 %copy-start.3 = (bf16[8,160,384]{2,1,0:T(8,128)(2,1)}, bf16[8,160,384]{2,1,0:T(8,128)(2,1)S(1)}, u32[]{:S(2)}) copy-start(bf16[8,160,384]{2,1,0:T(8,128)(2,1)S(1)} %all_to_all.74) | copy-start | bytes 2949124
  97.2 12.5 %all-to-all-start.3 = ((bf16[8,160,256]{2,1,0:T(8,128)(2,1)}), bf16[8,160,256]{2,1,0:T(8,128)(2,1)S(1)}, u32[]{:S(2)}, u32[]{:S(2)}) async-start(bf16[8,160,256]{2,1,0:T(8,128)(2,1)} %bitcast.33), calls=%async_computation.3 | async-start | bytes 1310720 | tf_op jit(solution)/shard_map/all_to_all | solution.py:326
  100.8 1.0 copy-start.8
  101.8 1.0 copy-start.9
  109.7 4.1 %copy-start.13 = (bf16[8,160,256]{2,1,0:T(8,128)(2,1)}, bf16[8,160,256]{2,1,0:T(8,128)(2,1)S(1)}, u32[]{:S(2)}) copy-start(bf16[8,160,256]{2,1,0:T(8,128)(2,1)S(1)} %all-to-all-done.3) | copy-start | bytes 1966084
  109.7 19.5 %all-to-all-start.2 = ((bf16[8,160,512]{2,1,0:T(8,128)(2,1)}), bf16[8,160,512]{2,1,0:T(8,128)(2,1)S(1)}, u32[]{:S(2)}, u32[]{:S(2)}) async-start(bf16[8,160,512]{2,1,0:T(8,128)(2,1)} %bitcast.10), calls=%async_computation.2 | async-start | bytes 2621440 | tf_op jit(solution)/shard_map/all_to_all | solution.py:331
  126.8 6.1 %copy-start.11 = (f32[16,512]{1,0:T(8,128)S(1)}, f32[16,512]{1,0:T(8,128)}, u32[]{:S(2)}) copy-start(f32[16,512]{1,0:T(8,128)} %copy-done.10) | copy-start | bytes 98308
  129.3 21.3 %all-to-all-start.4 = ((bf16[8,160,512]{2,1,0:T(8,128)(2,1)}), bf16[8,160,512]{2,1,0:T(8,128)(2,1)S(1)}, u32[]{:S(2)}, u32[]{:S(2)}) async-start(bf16[8,160,512]{2,1,0:T(8,128)(2,1)} %bitcast.42), calls=%async_computation.4 | async-start | bytes 2621440 | tf_op jit(solution)/shard_map/all_to_all | solution.py:342
  132.9 79.8 %reduce-scatter.2.cloned.1.call-start = ((), (), s32[]{:S(2)}) async-start(), calls=%async_computation.9 | async-start | bytes 2396160 | tf_op jit(solution)/shard_map/reduce_scatter | solution.py:366
  133.0 1.3 copy-start.6
  140.7 1.0 copy-start
  150.5 1.3 copy-start.1
  153.6 1.4 copy-start.12
Sparse Core Ops, SparseCore 0:
  10.7 64.2 all-gather.1
  153.7 58.8 reduce-scatter.1

commit v6 on v5

--- a/solution.py
+++ b/solution.py
@@ -316,7 +316,7 @@
         [lead, got, rank, gate],
         [pltpu.VMEM((GTOK, TAIL), BF), pltpu.VMEM((GTOK, WIDTH), BF), picked],
         flops=100 * square,
-        room=ROOM,
+        room=56,
     )
     exchange = functools.partial(
         lax.all_to_all, axis_name="lo", split_axis=0, concat_axis=0, tiled=True

time: 222 us -> 222 us (level)
  waiting for transfers between devices: 34.3 us -> 31.3 us
  Pallas kernels: 33.6 us -> 36.3 us
    pallas_call x7, Pallas kernels: 31.9 us -> 34.6 us  [call(): pl.pallas_call(kernel, out_shape=shapes, in_specs=[SMEM] * scalars + [VME...]
  transfers between devices with their start and end apart: 6 -> 6, of which waited for: 6 -> 6; matrix products, arithmetic and copies ran while one was open for 1% -> 1% of each run, Pallas kernels for 13% -> 14%
where the time goes in v6:
time: 222 us; the launch traced here: 221 us
  blocking collectives  113 us (51%)
  Pallas kernels  36.3 us (16%)
  waiting for transfers between devices  31.3 us (14%)
  starting transfers between devices  16.5 us (7%)
  between operations  14.2 us (6%)
  local copies, waits for them, and re-layouts  8.59 us (4%)
    all_gather x1, blocking collectives, body(): lead = lax.all_gather(lead_sent, 'hi', axis=0, tiled=True)  46.7 us
    pallas_call x7, Pallas kernels, call(): pl.pallas_call(kernel, out_shape=shapes, in_specs=[SMEM] * scalars + [VME...  34.6 us
    all_to_all x1, blocking collectives, body(): share = over_dp(weight_part).reshape(data, -1, WIDTH).astype(F32)  24.2 us
    all_to_all x1, blocking collectives, body(): over_dp(jnp.tile(share, (data, 1))).reshape(3, 1, WIDTH, WIDTH)  24.2 us
    all_to_all x1, blocking collectives, body(): rest = exchange(rows_rest)  18.2 us
    all_gather x1, waiting for transfers between devices, body(): got = lax.all_gather(rest_sent, 'hi', axis=0, tiled=True)  11 us
    reduce_scatter x1, waiting for transfers between devices, body(): lax.psum_scatter(partial.reshape(HI * BACK, LANES), 'hi', scatter_dimensi...  8.15 us
    all_to_all x1, waiting for transfers between devices, body(): ib = exchange(input_back)  7.46 us
  transfers between devices with their start and end apart: 6, of which 6 were waited for; matrix products, arithmetic and copies ran while one was open for 1% of the time, Pallas kernels for 14%

profile of v6, /device:TPU:6, one launch (start us, length us, event | category | flops | bytes accessed | tf_op | source)
XLA Modules:
  0.0 220.6 jit_solution(15472138028234564770)
XLA Ops:
  7.2 1.7 shard_map.118
  9.0 46.7 %all_gather.7.got.lead = bf16[3840,128]{1,0:T(8,128)(2,1)S(1)} all-gather(bf16[480,128]{1,0:T(8,128)(2,1)} %get-tuple-element.24), channel_id=1, replica_groups=mesh['dp'=8,'hi'=8,'lo'=8] {'hi'}, dimensions={0}, use_global_device_ids=true | all-gather | bytes 1105920 | tf_op jit(solution)/shard_map/all_gather | solution.py:303
  55.7 2.2 %shard_map.119 = (bf16[1280,384]{1,0:T(8,128)(2,1)}, f32[16,512]{1,0:T(8,128)S(1)}, f32[16,512]{1,0:T(8,128)S(1)}, f32[16,512]{1,0:T(8,128)S(1)}) custom-call(s32[1]{0:T(128)} %bitcast.first, bf16[3840,128]{1,0:T(8,128)(2,1)S(1)} %all_gather.7.got.lead), custom_call_target="tpu_custom_call" | custom-call | bytes 2064388 | tf_op jit(solution)/shard_map/pallas_call | solution.py:58
  59.2 4.3 %all-to-all-start = ((bf16[8,160,384]{2,1,0:T(8,128)(2,1)}), bf16[8,160,384]{2,1,0:T(8,128)(2,1)S(1)}, u32[]{:S(2)}, u32[]{:S(2)}) async-start(bf16[8,160,384]{2,1,0:T(8,128)(2,1)} %bitcast.3), calls=%async_computation | async-start | bytes 1966080 | tf_op jit(solution)/shard_map/all_to_all | solution.py:324
  63.5 11.0 %all-gather.2.cloned.1.call-done.got = bf16[4608,128]{1,0:T(8,128)(2,1)} async-done(((bf16[576,128]{1,0:T(8,128)(2,1)}), bf16[4608,128]{1,0:T(8,128)(2,1)}) %all-gather.2.cloned.1.call-update) | async-done | bytes 1179664 | tf_op jit(solution)/shard_map/all_gather | solution.py:302
  74.5 4.2 %shard_map.120 = (bf16[1280,384]{1,0:T(8,128)(2,1)}, bf16[1280,256]{1,0:T(8,128)(2,1)}) custom-call(bf16[3840,128]{1,0:T(8,128)(2,1)} %copy-done, bf16[4608,128]{1,0:T(8,128)(2,1)} %all-gather.2.cloned.1.call-done.got, f32[16,512]{1,0:T(8,128)} %copy-done.9, f32[16,512]{1,0:T(8,128)} %copy-done.11), custom_call_target="tpu_custom_call" | custom-call | flops 67108864000 | bytes 3866624 | tf_op jit(solution)/shard_map/pallas_call | solution.py:58
  79.5 18.2 %all_to_all.74 = bf16[8,160,384]{2,1,0:T(8,128)(2,1)S(1)} all-to-all(bf16[8,160,384]{2,1,0:T(8,128)(2,1)} %bitcast.41), channel_id=1, replica_groups=mesh['dp'=8,'hi'=8,'lo'=8] {'lo'}, dimensions={0} | all-to-all | bytes 1966080 | tf_op jit(solution)/shard_map/all_to_all | solution.py:325
  97.7 4.2 %all-to-all-start.3 = ((bf16[8,160,256]{2,1,0:T(8,128)(2,1)}), bf16[8,160,256]{2,1,0:T(8,128)(2,1)}, u32[]{:S(2)}, u32[]{:S(2)}) async-start(bf16[8,160,256]{2,1,0:T(8,128)(2,1)} %bitcast.42), calls=%async_computation.3 | async-start | bytes 1310720 | tf_op jit(solution)/shard_map/all_to_all | solution.py:326
  103.0 5.3 %shard_map.121 = bf16[1280,512]{1,0:T(8,128)(2,1)} custom-call(bf16[1280,384]{1,0:T(8,128)(2,1)S(1)} %bitcast.28, bf16[1280,384]{1,0:T(8,128)(2,1)S(1)} %bitcast.30, bf16[512,512]{1,0:T(8,128)(2,1)S(1)} %bitcast.33, bf16[512,512]{1,0:T(8,128)(2,1)S(1)} %bitcast.35, bf16[512,512]{1,0:T(8,128)(2,1)S(1)} %bitcast.37), custom_call_target="tpu_custom_call" | custom-call | flops 2013265920 | bytes 4849664 | tf_op jit(solution)/shard_map/pallas_call | solution.py:58
  108.4 2.4 %all-to-all-done.3 = bf16[8,160,256]{2,1,0:T(8,128)(2,1)} async-done(((bf16[8,160,256]{2,1,0:T(8,128)(2,1)}), bf16[8,160,256]{2,1,0:T(8,128)(2,1)}, u32[]{:S(2)}, u32[]{:S(2)}) %all-to-all-start.3) | async-done | bytes 655392 | tf_op jit(solution)/shard_map/all_to_all | solution.py:326
  110.7 3.6 %all-to-all-start.2 = ((bf16[8,160,512]{2,1,0:T(8,128)(2,1)}), bf16[8,160,512]{2,1,0:T(8,128)(2,1)S(1)}, u32[]{:S(2)}, u32[]{:S(2)}) async-start(bf16[8,160,512]{2,1,0:T(8,128)(2,1)} %bitcast.10), calls=%async_computation.2 | async-start | bytes 2621440 | tf_op jit(solution)/shard_map/all_to_all | solution.py:331
  114.3 13.0 %shard_map.122 = (bf16[1280,512]{1,0:T(8,128)(2,1)}, bf16[1536,512]{1,0:T(8,128)(2,1)}) custom-call(bf16[1280,384]{1,0:T(8,128)(2,1)} %bitcast.29, bf16[1280,384]{1,0:T(8,128)(2,1)} %bitcast.31, bf16[1280,256]{1,0:T(8,128)(2,1)} %bitcast.13.late, bf16[512,512]{1,0:T(8,128)(2,1)} %bitcast.32, bf16[512,512]{1,0:T(8,128)(2,1)} %bitcast.34, ...), custom_call_target="tpu_custom_call" | custom-call | flops 5368709120 | bytes 7077888 | tf_op jit(solution)/shard_map/pallas_call | solution.py:58
  127.3 1.4 all-to-all-done.2
  128.7 4.4 %all-to-all-start.4 = ((bf16[8,160,512]{2,1,0:T(8,128)(2,1)}), bf16[8,160,512]{2,1,0:T(8,128)(2,1)S(1)}, u32[]{:S(2)}, u32[]{:S(2)}) async-start(bf16[8,160,512]{2,1,0:T(8,128)(2,1)} %bitcast.40), calls=%async_computation.4 | async-start | bytes 2621440 | tf_op jit(solution)/shard_map/all_to_all | solution.py:342
  133.2 1.3 copy-done.5
  134.4 6.4 %shard_map.123 = (bf16[8,1040,128]{2,1,0:T(8,128)(2,1)}, bf16[1024,640]{1,0:T(8,128)(2,1)S(1)}) custom-call(s32[1]{0:T(128)} %bitcast.first, bf16[4608,128]{1,0:T(8,128)(2,1)S(1)} %copy-done.5, f32[16,512]{1,0:T(8,128)S(1)} %copy-done.10, f32[16,512]{1,0:T(8,128)S(1)} %get-tuple-element.26.ids, f32[16,512]{1,0:T(8,128)S(1)} %copy-done.12, ...), custom_call_target="tpu_custom_call" | custom-call | flops 2013265920 | bytes 6029316 | tf_op jit(solution)/shard_map/pallas_call | solution.py:58
  141.9 7.5 %all-to-all-done.4 = bf16[8,160,512]{2,1,0:T(8,128)(2,1)S(1)} async-done(((bf16[8,160,512]{2,1,0:T(8,128)(2,1)}), bf16[8,160,512]{2,1,0:T(8,128)(2,1)S(1)}, u32[]{:S(2)}, u32[]{:S(2)}) %all-to-all-start.4) | async-done | bytes 1310752 | tf_op jit(solution)/shard_map/all_to_all | solution.py:342
  149.4 1.3 copy-done.2
  150.7 1.7 shard_map.124
  152.4 1.4 copy-done.13
  153.8 24.2 %all_to_all.75 = bf16[8,192,512]{2,1,0:T(8,128)(2,1)S(1)} all-to-all(bf16[8,192,512]{2,1,0:T(8,128)(2,1)S(1)} %bitcast.39), channel_id=1, replica_groups=mesh['dp'=8,'hi'=8,'lo'=8] {'dp'}, dimensions={0} | all-to-all | bytes 3145728 | tf_op jit(solution)/shard_map/all_to_all | solution.py:373
  178.5 24.2 %all_to_all.76 = bf16[8,192,512]{2,1,0:T(8,128)(2,1)S(1)} all-to-all(bf16[8,192,512]{2,1,0:T(8,128)(2,1)S(1)} %tile.2), channel_id=1, replica_groups=mesh['dp'=8,'hi'=8,'lo'=8] {'dp'}, dimensions={0} | all-to-all | bytes 3145728 | tf_op jit(solution)/shard_map/all_to_all | solution.py:376
  203.9 8.1 %reduce-scatter.2.cloned.1.call-done.got = bf16[1040,128]{1,0:T(8,128)(2,1)} async-done(((bf16[8320,128]{1,0:T(8,128)(2,1)}), bf16[1040,128]{1,0:T(8,128)(2,1)}) %reduce-scatter.2.cloned.1.call-update) | async-done | bytes 266256 | tf_op jit(solution)/shard_map/reduce_scatter | solution.py:366
  212.0 1.7 shard_map.125
  (34 shorter events, 5.9 us)
Async XLA Ops:
  7.2 67.3 %all-gather.2.cloned.1.call-start = ((), (), s32[]{:S(2)}) async-start(), calls=%async_computation.8 | async-start | bytes 1327104 | tf_op jit(solution)/shard_map/all_gather | solution.py:302
  55.7 18.7 %copy-start = (bf16[3840,128]{1,0:T(8,128)(2,1)}, bf16[3840,128]{1,0:T(8,128)(2,1)S(1)}, u32[]{:S(2)}) copy-start(bf16[3840,128]{1,0:T(8,128)(2,1)S(1)} %all_gather.7.got.lead) | copy-start | bytes 2949124
  58.0 0.6 copy-start.9
  58.6 0.6 copy-start.11
  59.2 20.3 %all-to-all-start = ((bf16[8,160,384]{2,1,0:T(8,128)(2,1)}), bf16[8,160,384]{2,1,0:T(8,128)(2,1)S(1)}, u32[]{:S(2)}, u32[]{:S(2)}) async-start(bf16[8,160,384]{2,1,0:T(8,128)(2,1)} %bitcast.3), calls=%async_computation | async-start | bytes 1966080 | tf_op jit(solution)/shard_map/all_to_all | solution.py:324
  79.5 22.4 %copy-start.3 = (bf16[8,160,384]{2,1,0:T(8,128)(2,1)}, bf16[8,160,384]{2,1,0:T(8,128)(2,1)S(1)}, u32[]{:S(2)}) copy-start(bf16[8,160,384]{2,1,0:T(8,128)(2,1)S(1)} %all-to-all-done) | copy-start | bytes 2949124
  79.5 22.4 %copy-start.6 = (bf16[1,512,512]{2,1,0:T(8,128)(2,1)S(1)}, bf16[1,512,512]{2,1,0:T(8,128)(2,1)}, u32[]{:S(2)}) copy-start(bf16[1,512,512]{2,1,0:T(8,128)(2,1)} %param.11) | copy-start | bytes 1572868
  79.5 22.5 %copy-start.7 = (bf16[1,512,512]{2,1,0:T(8,128)(2,1)S(1)}, bf16[1,512,512]{2,1,0:T(8,128)(2,1)}, u32[]{:S(2)}) copy-start(bf16[1,512,512]{2,1,0:T(8,128)(2,1)} %param.12) | copy-start | bytes 1572868
  97.7 10.6 %copy-start.4 = (bf16[8,160,384]{2,1,0:T(8,128)(2,1)}, bf16[8,160,384]{2,1,0:T(8,128)(2,1)S(1)}, u32[]{:S(2)}) copy-start(bf16[8,160,384]{2,1,0:T(8,128)(2,1)S(1)} %all_to_all.74) | copy-start | bytes 2949124
  97.7 13.0 %all-to-all-start.3 = ((bf16[8,160,256]{2,1,0:T(8,128)(2,1)}), bf16[8,160,256]{2,1,0:T(8,128)(2,1)}, u32[]{:S(2)}, u32[]{:S(2)}) async-start(bf16[8,160,256]{2,1,0:T(8,128)(2,1)} %bitcast.42), calls=%async_computation.3 | async-start | bytes 1310720 | tf_op jit(solution)/shard_map/all_to_all | solution.py:326
  102.0 1.0 copy-start.8
  110.7 18.0 %all-to-all-start.2 = ((bf16[8,160,512]{2,1,0:T(8,128)(2,1)}), bf16[8,160,512]{2,1,0:T(8,128)(2,1)S(1)}, u32[]{:S(2)}, u32[]{:S(2)}) async-start(bf16[8,160,512]{2,1,0:T(8,128)(2,1)} %bitcast.10), calls=%async_computation.2 | async-start | bytes 2621440 | tf_op jit(solution)/shard_map/all_to_all | solution.py:331
  127.3 5.8 %copy-start.10 = (f32[16,512]{1,0:T(8,128)S(1)}, f32[16,512]{1,0:T(8,128)}, u32[]{:S(2)}) copy-start(f32[16,512]{1,0:T(8,128)} %copy-done.9) | copy-start | bytes 98308
  127.3 5.8 %copy-start.12 = (f32[16,512]{1,0:T(8,128)S(1)}, f32[16,512]{1,0:T(8,128)}, u32[]{:S(2)}) copy-start(f32[16,512]{1,0:T(8,128)} %copy-done.11) | copy-start | bytes 98308
  128.7 20.6 %all-to-all-start.4 = ((bf16[8,160,512]{2,1,0:T(8,128)(2,1)}), bf16[8,160,512]{2,1,0:T(8,128)(2,1)S(1)}, u32[]{:S(2)}, u32[]{:S(2)}) async-start(bf16[8,160,512]{2,1,0:T(8,128)(2,1)} %bitcast.40), calls=%async_computation.4 | async-start | bytes 2621440 | tf_op jit(solution)/shard_map/all_to_all | solution.py:342
  133.1 78.9 %reduce-scatter.2.cloned.1.call-start = ((), (), s32[]{:S(2)}) async-start(), calls=%async_computation.9 | async-start | bytes 2396160 | tf_op jit(solution)/shard_map/reduce_scatter | solution.py:366
  133.2 1.3 copy-start.5
  140.9 1.0 copy-start.1
  149.4 1.3 copy-start.2
  152.4 1.4 copy-start.13
Sparse Core Ops, SparseCore 0:
  10.7 63.7 all-gather.1
  152.6 59.4 reduce-scatter.1
